TPU v7x, 256 devices: a whole 4x4x8 slice. The times are simulated.
256 devices in a mesh: dp: 8 (over x, y_lo), ctx: 32 (over y_hi, z, core).
Axes of the slice: x: 4, y: 4 (y_hi: 2, y_lo: 2; y = y_hi * 2 + y_lo), z: 8, core: 2. Of those that a mesh axis runs over, the one named last changes fastest.
Arguments:
- sequence: bfloat16 [8, 8192, 2048], P('dp', 'ctx'), may hold values from -6 to 6
- n_blocks: int32 [8, 64], P('dp', 'ctx'), may hold values 0 or 1
- w_dt: float32 [2048, 32], replicated, may hold values from -0.125 to 0.125
- dt_bias: float32 [32], replicated, may hold values from -4 to -1
- decay_rate: float32 [32], replicated, may hold values from 2e-05 to 1
- w_b: float32 [2048, 64], replicated, may hold values from -0.015625 to 0.015625
- w_c: float32 [2048, 64], replicated, may hold values from -0.015625 to 0.015625
- d_skip: float32 [32], replicated, may hold values from 0.5 to 1.5
- cotangent: bfloat16 [8, 8192, 2048], P('dp', 'ctx'), may hold values from -6 to 6
Outputs:
- mixed: bfloat16 [8, 8192, 2048], P('dp', 'ctx')
- grad_sequence: bfloat16 [8, 8192, 2048], P('dp', 'ctx')
- grad_w_dt: float32 [2048, 32], replicated
- grad_dt_bias: float32 [32], replicated
- grad_decay_rate: float32 [32], replicated
- grad_w_b: float32 [2048, 64], replicated
- grad_w_c: float32 [2048, 64], replicated
- grad_d_skip: float32 [32], replicated
All inputs are finite; a program needn't handle non-finite values. No bound on the sum of `n_blocks` on one device may be relied on, other than what follows from the above.
Results may differ from a plain program's by a relative error of at most 0.001.
Values sent between devices are 32-bit elements; how exact they have to be, the bound alone decides.
A program may use at most 256 MiB of HBM per device.

v0:
```python
import jax
import jax.numpy as jnp
from jax import lax
from jax.sharding import PartitionSpec as P

BLOCK = 128


precise = lax.Precision.HIGHEST


def prefix(value, axis, join, neutral, backward):
    count, mine = (lax.axis_size(axis), lax.axis_index(axis))
    pieces = jax.tree.map(lambda part: lax.all_gather(part, axis), value)
    if backward:
        pieces = jax.tree.map(lambda part: part[::-1], pieces)
        mine = count - 1 - mine
    total = jax.tree.map(
        lambda part, zero: jnp.full_like(part, 0) + jnp.asarray(zero, part.dtype), value, neutral
    )

    def turn(position, total):
        longer = join(total, jax.tree.map(lambda part: part[position], pieces))
        return jax.tree.map(lambda new, old: jnp.where(position < mine, new, old), longer, total)

    return lax.fori_loop(0, count - 1, turn, total)


def strand_pieces(values, keep, params):
    w_dt, dt_bias, decay_rate, w_b, w_c, d_skip = params
    length, width = values.shape
    heads = w_dt.shape[1]
    head_size = width // heads
    count = length // BLOCK
    steps = (
        jax.nn.softplus(jnp.einsum("ld,dh->hl", values, w_dt, precision=precise) + dt_bias[:, None])
        * keep[None, :]
    )
    b_rows = jnp.dot(values, w_b, precision=precise)
    c_rows = jnp.dot(values, w_c, precision=precise)
    log_decay = -steps * decay_rate[:, None]
    step_cols = jnp.repeat(steps.T, head_size, axis=1)
    inputs = (step_cols * values).reshape(count, BLOCK, width)
    within = jnp.cumsum(log_decay.reshape(heads, count, BLOCK), axis=2).transpose(1, 0, 2)
    b_blocks = b_rows.reshape(count, BLOCK, b_rows.shape[1])
    c_blocks = c_rows.reshape(count, BLOCK, c_rows.shape[1])
    causal = jnp.arange(BLOCK)[:, None] >= jnp.arange(BLOCK)[None, :]

    def advance(state, block_data):
        cum_k, b_k, c_k, u_k = block_data
        diff = cum_k[:, :, None] - cum_k[:, None, :]
        scores = jnp.dot(c_k, b_k.T, precision=precise)
        mixing = scores[None, :, :] * jnp.exp(jnp.where(causal[None, :, :], diff, -1e30))
        inner = jnp.einsum(
            "hts,shp->thp", mixing, u_k.reshape(BLOCK, heads, head_size), precision=precise
        ).reshape(BLOCK, width)
        cum_cols = jnp.repeat(cum_k.T, head_size, axis=1)
        from_state = jnp.exp(cum_cols) * jnp.dot(c_k, state, precision=precise)
        last = cum_cols[-1]
        tail = jnp.exp(last[None, :] - cum_cols)
        new_state = jnp.exp(last)[None, :] * state + jnp.dot(b_k.T, tail * u_k, precision=precise)
        return (new_state, inner + from_state)

    start = jnp.zeros((w_b.shape[1], width), jnp.float32)
    final, outputs = lax.scan(advance, start, (within, b_blocks, c_blocks, inputs))
    skip = jnp.repeat(d_skip, head_size)
    local_out = outputs.reshape(length, width) + skip[None, :] * values
    totals = within[:, :, -1]
    offsets = jnp.cumsum(totals, axis=0) - totals
    running = (within + offsets[:, :, None]).transpose(1, 0, 2).reshape(heads, length)
    decay_all = jnp.repeat(jnp.exp(jnp.sum(totals, axis=0)), head_size)
    return (local_out, decay_all, final, jnp.exp(running), c_rows)


def correction(decay_run, c_rows, carried):
    heads = decay_run.shape[0]
    head_size = carried.shape[1] // heads
    moved = jnp.dot(c_rows, carried, precision=precise)
    return jnp.repeat(decay_run.T, head_size, axis=1) * moved


def combine(earlier, later):
    return (earlier[0] * later[0], later[0][None, :] * earlier[1] + later[1])


def carry_upward(decay, state):
    start = (jnp.ones_like(decay), jnp.zeros_like(state))
    return prefix((decay, state), "ctx", combine, start, False)[1]


def carry_downward(decay, state):
    start = (jnp.ones_like(decay), jnp.zeros_like(state))
    return prefix((decay, state), "ctx", combine, start, True)[1]


def strand_grads(values, keep, params, cot_rows, upward):

    def local_part(inputs, weights):
        return strand_pieces(inputs, keep, weights)

    pieces, pull_local = jax.vjp(local_part, values, params)
    local_out, decay, state, decay_run, c_rows = pieces
    carried = carry_upward(decay, state) if upward else carry_downward(decay, state)
    extra, pull_corr = jax.vjp(correction, decay_run, c_rows, carried)
    d_run, d_crows, from_later = pull_corr(cot_rows)
    adjoint = carry_downward(decay, from_later) if upward else carry_upward(decay, from_later)
    d_decay = jnp.sum(adjoint * carried, axis=0)
    d_values, d_params = pull_local((cot_rows, d_decay, adjoint, d_run, d_crows))
    return (local_out + extra, d_values, d_params)


def on_device(sequence, n_blocks, w_dt, dt_bias, decay_rate, w_b, w_c, d_skip, cotangent):
    params = (w_dt, dt_bias, decay_rate, w_b, w_c, d_skip)
    values = sequence[0].astype(jnp.float32)
    keep = jnp.repeat(1.0 - n_blocks[0].astype(jnp.float32), BLOCK)
    cot_rows = cotangent[0].astype(jnp.float32)
    out_fwd, dval_fwd, dpar_fwd = strand_grads(values, keep, params, cot_rows, True)
    out_rev, dval_rev, dpar_rev = strand_grads(
        values[::-1, ::-1], keep[::-1], params, cot_rows[::-1, ::-1], False
    )
    mixed = (out_fwd + out_rev[::-1, ::-1]).astype(jnp.bfloat16)[None]
    grad_seq = (dval_fwd + dval_rev[::-1, ::-1]).astype(jnp.bfloat16)[None]
    totals = jax.tree.map(lambda first, second: first + second, dpar_fwd, dpar_rev)
    grad_dt, grad_bias, grad_rate, grad_b, grad_c, grad_skip = totals
    matrices = jnp.concatenate([grad_dt, grad_b, grad_c], axis=1)
    vectors = jnp.stack([grad_bias, grad_rate, grad_skip])
    matrices, vectors = lax.psum((matrices, vectors), ("dp", "ctx"))
    heads = w_dt.shape[1]
    state_dim = w_b.shape[1]
    return (
        mixed,
        grad_seq,
        matrices[:, :heads],
        vectors[0],
        vectors[1],
        matrices[:, heads : heads + state_dim],
        matrices[:, heads + state_dim :],
        vectors[2],
    )


def solution(mesh):
    return jax.shard_map(
        on_device,
        mesh=mesh,
        in_specs=(
            P("dp", "ctx", None),
            P("dp", "ctx"),
            P(),
            P(),
            P(),
            P(),
            P(),
            P(),
            P("dp", "ctx", None),
        ),
        out_specs=(P("dp", "ctx", None), P("dp", "ctx", None), P(), P(), P(), P(), P(), P()),
        check_vma=False,
    )
```

profile of v0, /device:TPU:1, one launch (start us, length us, event | category | flops | bytes accessed | tf_op | source)
XLA Modules:
  0.0 1318.6 jit_solution(10644873209559208998)
XLA Ops:
  10.1 15.0 %rev.27 = f32[256,2048]{1,0:T(8,128)S(1)} reverse(f32[256,2048]{1,0:T(8,128)} %bitcast_convert_fusion), dimensions={0,1} | reverse | bytes 4194304 | tf_op jit(solution)/shard_map/rev | solution.py:119
  31.8 3.0 copy.381
  36.4 14.9 %rev.34 = f32[256,2048]{1,0:T(8,128)S(1)} reverse(f32[256,2048]{1,0:T(8,128)} %convert_bitcast_fusion), dimensions={0,1} | reverse | bytes 4194304 | tf_op jit(solution)/shard_map/rev | solution.py:119
  51.3 4.6 fusion.176
  57.8 3.1 copy.373
  60.8 3.2 mul.744
  84.0 67.6 %while.193 = (s32[]{:T(128)}, f32[64,2048]{1,0:T(8,128)S(1)}, f32[2,128,2048]{2,1,0:T(8,128)}, f32[2,64,128]{2,1,0:T(8,128)}, f32[2,32,128,128]{3,2,1,0:T(8,128)...) while((s32[]{:T(128)}, f32[64,2048]{1,0:T(8,128)S(1)}, ...), condition=%wide.region_9.11_spmd.clone.clone, body=%wide.region_8.10_spmd.clone.clone.sunk | while | flops 823001088 | bytes 87562544 | solution.py:65
  89.0 3.1 multiply_dynamic-update-slice_fusion.11
  93.0 5.1 fusion.396
  104.2 4.0 bitcast_dynamic-update-slice_fusion.27
  122.8 3.0 multiply_dynamic-update-slice_fusion.11
  126.7 5.1 fusion.396
  137.9 4.0 bitcast_dynamic-update-slice_fusion.27
  152.9 50.0 %all-gather.5 = f32[32,1,2048]{2,1,0:T(1,128)} all-gather(f32[1,1,2048]{2,1,0:T(1,128)S(1)} %reshape.867), channel_id=1, replica_groups=mesh['dp'=8,'ctx'=32] {'ctx'}, dimensions={0}, use_global_device_ids=true | all-gather | bytes 270336 | tf_op jit(solution)/shard_map/all_gather | solution.py:14
  204.0 4.9 rev.29
  214.2 47.5 %while.191 = (s32[]{:T(128)}, f32[64,2048]{1,0:T(8,128)S(1)}, s32[]{:T(128)}, f32[32,2048]{1,0:T(8,128)S(1)}, f32[32,64,2048]{2,1,0:T(8,128)}, /*index=5*/s32[]{:T(128)}, s32[]{:T(128)}) while((s32[]{:T(128)}, f32[64,2048]{1,0:T(8,128)S(1)}, s32[]{:T(128)}, f32[32,2048]{1,0:T(8,128)S(1)}, f32[32,64,2048]{2,1,0:T(8,128)}, ...), condition=%wide.region_32.34_spmd.clone, body=%wide.region_31.33_spmd.clone.sunk | while | flops 524292 | bytes 1597545 | solution.py:26
  265.2 92.6 %while.187 = (s32[]{:T(128)}, f32[64,2048]{1,0:T(8,128)S(1)}, f32[2,32,128]{2,0,1:T(2,128)}, f32[2,128,64]{1,0,2:T(2,128)}, f32[2,128,64]{1,0,2:T(2,128)}, /*ind...) while((s32[]{:T(128)}, f32[64,2048]{1,0:T(8,128)S(1)}, ...), condition=%wide.region_40.42_spmd.clone, body=%wide.region_33.41_spmd.clone.sunk | while | flops 1643905024 | bytes 73060888 | solution.py:65
  274.9 4.9 fusion.379
  287.1 3.7 bitcast_add_fusion.15
  295.6 5.9 fusion.373
  320.8 4.9 fusion.379
  333.1 4.0 bitcast_add_fusion.15
  341.8 5.9 fusion.373
  357.8 11.7 rev.30
  369.6 72.8 %while.189 = (s32[]{:T(128)}, f32[64,2048]{1,0:T(8,128)S(1)}, s32[]{:T(128)}, f32[32,2048]{1,0:T(8,128)}, f32[32,64,2048]{2,1,0:T(8,128)}, /*index=5*/s32[]{:T(128)}, s32[]{:T(128)}) while((s32[]{:T(128)}, f32[64,2048]{1,0:T(8,128)S(1)}, s32[]{:T(128)}, f32[32,2048]{1,0:T(8,128)}, f32[32,64,2048]{2,1,0:T(8,128)}, ...), condition=%wide.region_13.15_spmd.clone, body=%wide.region_12.14_spmd.clone.sunk | while | flops 524292 | bytes 1597545 | solution.py:26
  443.7 10.5 multiply_reduce_fusion
  454.2 2.9 copy.408
  471.2 4.3 copy.364
  475.5 3.3 convert_multiply_fusion.1
  496.6 70.2 %while.192 = (s32[]{:T(128)}, f32[64,2048]{1,0:T(8,128)S(1)}, f32[2,128,2048]{2,1,0:T(8,128)}, f32[2,64,128]{2,1,0:T(8,128)S(1)}, f32[2,32,128,128]{3,2,1,0:T(8,...) while((s32[]{:T(128)}, f32[64,2048]{1,0:T(8,128)S(1)}, ...), condition=%wide.region_2.4_spmd.clone.clone, body=%wide.region_1.3_spmd.clone.clone.sunk | while | flops 823001088 | bytes 87497008 | solution.py:65
  502.9 3.1 multiply_dynamic-update-slice_fusion.9
  506.8 5.1 fusion.389
  518.8 4.0 bitcast_dynamic-update-slice_fusion.23
  537.9 3.0 multiply_dynamic-update-slice_fusion.9
  541.8 5.1 fusion.389
  553.8 4.0 bitcast_dynamic-update-slice_fusion.23
  569.5 3.0 copy.371
  572.5 4.0 fusion.179
  579.9 37.4 %all-gather.4 = f32[32,1,2048]{2,1,0:T(1,128)S(1)} all-gather(f32[1,1,2048]{2,1,0:T(1,128)S(1)} %reshape.865), channel_id=1, replica_groups=mesh['dp'=8,'ctx'=32] {'ctx'}, dimensions={0}, use_global_device_ids=true | all-gather | bytes 270336 | tf_op jit(solution)/shard_map/all_gather | solution.py:14
  617.4 5.3 rev.32
  622.7 2.9 copy.387
  625.7 17.7 %rev.31 = f32[256,2048]{1,0:T(8,128)} reverse(f32[256,2048]{1,0:T(8,128)} %get-tuple-element.2999), dimensions={0,1} | reverse | bytes 4194304 | tf_op jit(solution)/shard_map/rev | solution.py:121
  643.5 3.8 convolution_add_fusion.17
  651.3 3.2 convolution_add_fusion.8
  654.5 17.7 %rev.35 = f32[256,2048]{1,0:T(8,128)} reverse(f32[256,2048]{1,0:T(8,128)} %convolution_add_fusion.8), dimensions={0,1} | reverse | bytes 4194304 | tf_op jit(solution)/shard_map/rev | solution.py:122
  672.8 27.4 %all-gather.11.cloned.1.call-done = f32[2048,2048]{1,0:T(8,128)} async-done(((f32[64,2048]{1,0:T(8,128)}), f32[2048,2048]{1,0:T(8,128)}) %all-gather.11.cloned.1.call-update) | async-done | bytes 16777232 | tf_op jit(solution)/shard_map/all_gather | solution.py:14
  700.2 72.8 %while.188 = (s32[]{:T(128)}, f32[64,2048]{1,0:T(8,128)S(1)}, s32[]{:T(128)}, f32[32,2048]{1,0:T(8,128)}, f32[32,64,2048]{2,1,0:T(8,128)}, /*index=5*/s32[]{:T(128)}, s32[]{:T(128)}) while((s32[]{:T(128)}, f32[64,2048]{1,0:T(8,128)S(1)}, s32[]{:T(128)}, f32[32,2048]{1,0:T(8,128)}, f32[32,64,2048]{2,1,0:T(8,128)}, ...), condition=%wide.region_6.8_spmd.clone, body=%wide.region_5.7_spmd.clone.sunk | while | flops 524292 | bytes 1597545 | solution.py:26
  773.0 64.8 %all-gather.15.cloned.1.call-done = f32[2048,2048]{1,0:T(8,128)} async-done(((f32[64,2048]{1,0:T(8,128)}), f32[2048,2048]{1,0:T(8,128)}) %all-gather.15.cloned.1.call-update) | async-done | bytes 16777232 | tf_op jit(solution)/shard_map/all_gather | solution.py:14
  837.9 11.7 rev.33
  849.5 72.6 %while.190 = (s32[]{:T(128)}, f32[64,2048]{1,0:T(8,128)S(1)}, s32[]{:T(128)}, f32[32,2048]{1,0:T(8,128)}, f32[32,64,2048]{2,1,0:T(8,128)}, /*index=5*/s32[]{:T(128)}, s32[]{:T(128)}) while((s32[]{:T(128)}, f32[64,2048]{1,0:T(8,128)S(1)}, s32[]{:T(128)}, f32[32,2048]{1,0:T(8,128)}, f32[32,64,2048]{2,1,0:T(8,128)}, ...), condition=%wide.region_15.17_spmd.clone, body=%wide.region_14.16_spmd.clone.sunk | while | flops 524292 | bytes 1597545 | solution.py:26
  926.4 90.3 %while.186 = (s32[]{:T(128)}, f32[64,2048]{1,0:T(8,128)S(1)}, f32[2,32,128]{2,0,1:T(2,128)}, f32[2,128,64]{1,0,2:T(2,128)}, f32[2,128,64]{1,0,2:T(2,128)}, /*ind...) while((s32[]{:T(128)}, f32[64,2048]{1,0:T(8,128)S(1)}, ...), condition=%wide.region_23.25_spmd.clone, body=%wide.region_16.24_spmd.clone.sunk | while | flops 1643905024 | bytes 73060888 | solution.py:65
  935.8 4.9 fusion.358
  948.0 3.7 bitcast_add_fusion.14
  956.5 5.9 fusion.352
  980.8 4.9 fusion.358
  993.0 3.7 bitcast_add_fusion.14
  1001.5 5.9 fusion.352
  1016.8 4.3 copy.390
  1021.1 9.1 fusion.183
  1030.2 2.9 copy.392
  1035.7 3.9 reshape.834
  1054.4 75.8 %psum.15 = f32[3,32]{1,0:T(4,128)S(1)} all-reduce(f32[3,32]{1,0:T(4,128)S(1)} %pad_maximum_fusion.1), channel_id=1, replica_groups=mesh['dp'=8,'ctx'=32] {'dp','ctx'}, use_global_device_ids=true, to_apply=%region_57.59 | all-reduce | flops 96 | bytes 768 | tf_op jit(solution)/shard_map/psum | solution.py:127
  1134.5 2.9 fusion.155
  1137.4 170.2 %all-reduce.6.cloned.1.call-done = f32[2048,160]{0,1:T(8,128)} async-done(((f32[2048,160]{0,1:T(8,128)}), f32[2048,160]{0,1:T(8,128)}) %all-reduce.6.cloned.1.call-update) | async-done | bytes 1310736 | tf_op jit(solution)/shard_map/psum | solution.py:127
  (919 shorter events, 592.1 us)
Async XLA Ops:
  7.2 20.2 %copy-start = (f32[2048,64]{0,1:T(8,128)S(1)}, f32[2048,64]{0,1:T(8,128)}, u32[]{:S(2)}) copy-start(f32[2048,64]{0,1:T(8,128)} %param.32) | copy-start | bytes 1572868
  7.2 207.0 %all-gather.17.cloned.1.call-start = ((), (), s32[]{:S(2)}) async-start(), calls=%async_computation.4 | async-start | bytes 17301504 | tf_op jit(solution)/shard_map/all_gather | solution.py:14
  10.1 15.0 %copy-start.123 = (s32[1,2]{1,0:T(1,128)S(1)}, s32[1,2]{1,0:T(1,128)}, u32[]{:S(2)}) copy-start(s32[1,2]{1,0:T(1,128)} %param.27) | copy-start | bytes 28
  10.1 15.2 %copy-start.51 = (f32[2048,32]{0,1:T(8,128)S(1)}, f32[2048,32]{0,1:T(8,128)}, u32[]{:S(2)}) copy-start(f32[2048,32]{0,1:T(8,128)} %param.28) | copy-start | bytes 786436
  10.1 15.2 %copy-start.117 = (f32[32]{0:T(128)S(1)}, f32[32]{0:T(128)}, u32[]{:S(2)}) copy-start(f32[32]{0:T(128)} %param.29) | copy-start | bytes 388
  29.4 26.8 %copy-start.65 = (f32[256,64]{0,1:T(8,128)}, f32[256,64]{0,1:T(8,128)S(1)}, u32[]{:S(2)}) copy-start(f32[256,64]{0,1:T(8,128)S(1)} %fusion.226) | copy-start | bytes 196612
  30.2 4.6 copy-start.103
  51.3 4.6 copy-start.1
  55.9 301.9 %all-gather.13.cloned.1.call-start = ((), (), s32[]{:S(2)}) async-start(), calls=%async_computation.2 | async-start | bytes 17301504 | tf_op jit(solution)/shard_map/all_gather | solution.py:14
  151.6 61.5 %copy-start.55 = (f32[2,32,128]{2,1,0:T(8,128)}, f32[2,32,128]{2,1,0:T(8,128)S(1)}, u32[]{:S(2)}) copy-start(f32[2,32,128]{2,1,0:T(8,128)S(1)} %get-tuple-element.4113) | copy-start | bytes 98308
  151.6 58.7 %copy-start.18 = (bf16[1,256,2048]{2,1,0:T(8,128)(2,1)S(1)}, bf16[1,256,2048]{2,1,0:T(8,128)(2,1)}, u32[]{:S(2)}) copy-start(bf16[1,256,2048]{2,1,0:T(8,128)(2,1)} %param.26) | copy-start | bytes 3145732
  151.6 59.9 %copy-start.118 = (f32[32]{0:T(128)S(1)}, f32[32]{0:T(128)}, u32[]{:S(2)}) copy-start(f32[32]{0:T(128)} %param.29) | copy-start | bytes 388
  152.5 59.0 %copy-start.52 = (f32[2048,32]{0,1:T(8,128)S(1)}, f32[2048,32]{0,1:T(8,128)}, u32[]{:S(2)}) copy-start(f32[2048,32]{0,1:T(8,128)} %param.28) | copy-start | bytes 786436
  152.5 547.7 %all-gather.11.cloned.1.call-start = ((), (), s32[]{:S(2)}) async-start(), calls=%async_computation.1 | async-start | bytes 17301504 | tf_op jit(solution)/shard_map/all_gather | solution.py:14
  152.7 60.4 %copy-start.119 = (f32[32]{0:T(128)}, f32[32]{0:T(128)S(1)}, u32[]{:S(2)}) copy-start(f32[32]{0:T(128)S(1)} %slice_reduce_fusion.2) | copy-start | bytes 388
  202.9 10.2 copy-start.42
  271.1 11.2 copy-start.6
  290.8 4.8 copy-start.16
  301.5 5.1 copy-start.82
  303.0 6.1 copy-start.69
  303.0 6.3 copy-start.90
  306.8 4.7 copy-start.83
  317.0 11.2 copy-start.6
  337.0 4.8 copy-start.16
  347.7 5.0 copy-start.82
  349.2 6.1 copy-start.69
  349.2 6.3 copy-start.90
  353.0 4.6 copy-start.83
  357.8 11.7 copy-start.28
  369.5 74.1 %copy-start.3 = (f32[2,128,2048]{2,1,0:T(8,128)S(1)}, f32[2,128,2048]{2,1,0:T(8,128)}, u32[]{:S(2)}) copy-start(f32[2,128,2048]{2,1,0:T(8,128)} %get-tuple-element.4099) | copy-start | bytes 6291460
  369.5 74.1 %copy-start.66 = (f32[256,64]{0,1:T(8,128)S(1)}, f32[256,64]{0,1:T(8,128)}, u32[]{:S(2)}) copy-start(f32[256,64]{0,1:T(8,128)} %copy-done.65) | copy-start | bytes 196612
  369.5 74.1 %copy-start.96 = (f32[2048]{0:T(1024)S(1)}, f32[2048]{0:T(1024)}, u32[]{:S(2)}) copy-start(f32[2048]{0:T(1024)} %mul.737) | copy-start | bytes 24580
  442.4 11.8 copy-start.29
  443.7 15.4 %copy-start.104 = (f32[2,32]{1,0:T(2,128)S(1)}, f32[2,32]{1,0:T(2,128)}, u32[]{:S(2)}) copy-start(f32[2,32]{1,0:T(2,128)} %copy-done.103) | copy-start | bytes 772
  461.9 4.4 copy-start.78
  461.9 4.4 copy-start.81
  461.9 4.4 copy-start.108
  461.9 4.4 copy-start.111
  461.9 4.4 copy-start.113
  492.1 4.6 copy-start.13
  567.7 270.2 %all-gather.15.cloned.1.call-start = ((), (), s32[]{:S(2)}) async-start(), calls=%async_computation.3 | async-start | bytes 17301504 | tf_op jit(solution)/shard_map/all_gather | solution.py:14
  576.6 731.1 %all-reduce.6.cloned.1.call-start = ((), (), s32[]{:S(2)}) async-start(), calls=%async_computation | async-start | bytes 2621440 | tf_op jit(solution)/shard_map/psum | solution.py:127
  617.4 8.3 copy-start.61
  625.7 17.8 %copy-start.102 = (f32[2048]{0:T(1024)S(1)}, f32[2048]{0:T(1024)}, u32[]{:S(2)}) copy-start(f32[2048]{0:T(1024)} %get-tuple-element.2996) | copy-start | bytes 24580
  625.7 17.8 %copy-start.4 = (f32[2,128,2048]{2,1,0:T(8,128)S(1)}, f32[2,128,2048]{2,1,0:T(8,128)}, u32[]{:S(2)}) copy-start(f32[2,128,2048]{2,1,0:T(8,128)} %get-tuple-element.4099) | copy-start | bytes 6291460
  625.7 17.8 %copy-start.84 = (f32[2,128,64]{1,0,2:T(2,128)S(1)}, f32[2,128,64]{1,0,2:T(2,128)}, u32[]{:S(2)}) copy-start(f32[2,128,64]{1,0,2:T(2,128)} %get-tuple-element.1850) | copy-start | bytes 196612
  654.4 45.7 %copy-start.31 = (f32[64,2048]{1,0:T(8,128)S(1)}, f32[64,2048]{1,0:T(8,128)}, u32[]{:S(2)}) copy-start(f32[64,2048]{1,0:T(8,128)} %custom-call) | copy-start | bytes 1572868
  773.0 149.2 %copy-start.32 = (f32[64,2048]{1,0:T(8,128)}, f32[64,2048]{1,0:T(8,128)S(1)}, u32[]{:S(2)}) copy-start(f32[64,2048]{1,0:T(8,128)S(1)} %get-tuple-element.1813) | copy-start | bytes 1572868
  932.0 11.1 copy-start.7
  951.7 4.8 copy-start.17
  963.9 5.3 copy-start.73
  963.9 5.5 copy-start.93
  966.9 4.6 copy-start.86
  977.0 11.1 copy-start.7
  996.7 4.8 copy-start.17
  1008.8 5.3 copy-start.73
  1008.8 5.5 copy-start.93
  1011.8 4.6 copy-start.86
  1016.7 4.3 copy-start.21
  1016.7 4.3 copy-start.33
  1039.6 4.9 copy-start.79
  1039.6 4.9 copy-start.109
  1039.6 4.9 copy-start.114
  1052.9 77.4 %copy-start.46 = (f32[256,2048]{1,0:T(8,128)S(1)}, f32[256,2048]{1,0:T(8,128)}, u32[]{:S(2)}) copy-start(f32[256,2048]{1,0:T(8,128)} %get-tuple-element.3006) | copy-start | bytes 6291460
  (105 other events, 283.2 us)
Sparse Core Ops, SparseCore 0:
  56.0 143.0 all-gather.16
  201.9 134.5 all-gather.12
  567.8 132.3 all-gather.10
  703.4 134.4 all-gather.14
  1054.3 253.3 all-reduce.5
where the time goes:
time: 1340 us; the launch traced here: 1320 us
  local copies, waits for them, and re-layouts  407 us (30%)
  other arithmetic  276 us (21%)
  waiting for transfers between devices  263 us (20%)
  matrix products  189 us (14%)
  blocking collectives  163 us (12%)
  between operations  15.4 us (1%)
    select_n x124, other arithmetic, turn(): jnp.where(position < mine, new, old)  183 us
    psum x1, waiting for transfers between devices, on_device(): matrices, vectors = lax.psum((matrices, vectors), ('dp', 'ctx'))  170 us
    all_gather x4, waiting for transfers between devices, prefix(): pieces = jax.tree.map(lambda part: lax.all_gather(part, axis), value)  92.3 us
    all_gather x2, blocking collectives, prefix(): pieces = jax.tree.map(lambda part: lax.all_gather(part, axis), value)  87.4 us
    dynamic_slice x124, local copies, waits for them, and re-layouts, turn(): longer = join(total, jax.tree.map(lambda part: part[position], pieces))  79.9 us
    psum x1, blocking collectives, on_device(): matrices, vectors = lax.psum((matrices, vectors), ('dp', 'ctx'))  75.8 us
    dot_general x12, matrix products, advance(): jnp.einsum('hts,shp->thp', mixing, u_k.reshape(BLOCK, heads, head_size),...  63.5 us
    dynamic_slice x34, local copies, waits for them, and re-layouts, strand_pieces(): lax.scan(advance, start, (within, b_blocks, c_blocks, inputs))  43.6 us
  transfers between devices with their start and end apart: 5, of which 3 were waited for; matrix products, arithmetic and copies ran while one was open for 29% of the time, Pallas kernels for 0%

commit v1 on v0

v1 whole, which is shorter than its diff:
```python
import functools

import jax
import jax.numpy as jnp
from jax import lax
from jax.experimental import pallas as pl
from jax.experimental.pallas import tpu as pltpu
from jax.sharding import PartitionSpec as P

F32 = jnp.float32
BF16 = jnp.bfloat16
BLOCK = 128
T = 256
D = 2048
H = 32
N = 64
G = 16
MESH = pl.DeviceIdType.MESH
VMEM = pl.BlockSpec(memory_space=pltpu.VMEM)
SMEM = pl.BlockSpec(memory_space=pltpu.SMEM)
LIMIT = 48 * 1024 * 1024
RATIO = 3
FAR = -1e30


def iota(shape, axis):
    return lax.broadcasted_iota(jnp.int32, shape, axis)


def mat(a, b):
    return lax.dot_general(a, b, (((1,), (0,)), ((), ())), preferred_element_type=F32)


def mat_nt(a, b):
    return lax.dot_general(a, b, (((1,), (1,)), ((), ())), preferred_element_type=F32)


def split2(a):
    hi = a.astype(BF16)
    return hi, (a - hi.astype(F32)).astype(BF16)


def split3(a):
    hi = a.astype(BF16)
    rest = a - hi.astype(F32)
    mid = rest.astype(BF16)
    return hi, mid, (rest - mid.astype(F32)).astype(BF16)


def mat2(a, exact):
    hi, lo = split2(a)
    return mat(hi, exact) + mat(lo, exact)


def mat3(a, b):
    ah, al = split2(a)
    bh, bl = split2(b)
    return mat(ah, bh) + (mat(al, bh) + mat(ah, bl))


def mat3_nt(a, b):
    ah, al = split2(a)
    bh, bl = split2(b)
    return mat_nt(ah, bh) + (mat_nt(al, bh) + mat_nt(ah, bl))


def exact_left(zero_one, a):
    hi, mid, lo = split3(a)
    return mat(zero_one, hi) + (mat(zero_one, mid) + mat(zero_one, lo))


def exact_right(a, zero_one):
    hi, mid, lo = split3(a)
    return mat(hi, zero_one) + (mat(mid, zero_one) + mat(lo, zero_one))


def ones_where(condition):
    return jnp.where(condition, 1.0, 0.0).astype(BF16)


def flip_rows():
    return ones_where(iota((128, 128), 0) + iota((128, 128), 1) == 127)


def keep_column(nb_ref):
    first = 1.0 - nb_ref[0, 0].astype(F32)
    second = 1.0 - nb_ref[0, 1].astype(F32)
    return jnp.where(iota((T, 1), 0) < BLOCK, first, second)


def spread(j, width):
    rows = iota((128, 2 * width), 0)
    cols = iota((128, 2 * width), 1)
    head = j * (width // N) + (cols % width) // N
    return ones_where(rows == head + jnp.where(cols < width, 0, H))


def front_kernel(x_ref, dy_ref, nb_ref, wdt_ref, wb_ref, wc_ref, prm_ref,
                 pack_ref, c_ref, step_ref, z_ref, at_ref, bcf_ref, bcr_ref, whi_ref, wlo_ref):
    flip = flip_rows()
    pick = iota((128, 128), 0)
    cols = iota((128, 128), 1)
    swap = ones_where((pick < H) & (pick + cols == 2 * H - 1))

    def cut(i, carry):
        rows = pl.ds(pl.multiple_of(i * 128, 128), 128)
        dt = jnp.concatenate([wdt_ref[rows, :], jnp.zeros((128, 96), F32)], axis=1)
        bc = jnp.concatenate([wb_ref[rows, :], wc_ref[rows, :]], axis=1)
        dt_hi, dt_lo = split2(dt)
        bc_hi, bc_lo = split2(bc)
        whi_ref[rows, 0:128] = dt_hi
        wlo_ref[rows, 0:128] = dt_lo
        whi_ref[rows, 128:256] = bc_hi
        wlo_ref[rows, 128:256] = bc_lo
        return carry

    lax.fori_loop(0, G, cut, 0)

    def turned(ref, i):
        rows = pl.ds(pl.multiple_of((G - 1 - i) * 128, 128), 128)
        return mat(flip, ref[rows, 0:256]).astype(BF16)

    def mirror(i, carry):
        for ref in (whi_ref, wlo_ref):
            low = pl.ds(pl.multiple_of(i * 128, 128), 128)
            high = pl.ds(pl.multiple_of((G - 1 - i) * 128, 128), 128)
            for_low = turned(ref, i)
            for_high = turned(ref, G - 1 - i)
            for rows, got in ((low, for_low), (high, for_high)):
                ref[rows, 256:384] = got[:, 128:256]
                ref[rows, 0:128] = (
                    ref[rows, 0:128].astype(F32) + mat(got[:, 0:128], swap)
                ).astype(BF16)
        return carry

    lax.fori_loop(0, G // 2, mirror, 0)

    x = x_ref[...]
    proj = mat(x, whi_ref[...]) + mat(x, wlo_ref[...])
    lane = iota((T, 128), 1)
    z = proj[:, 0:128] + prm_ref[0:1, :]
    soft = jnp.maximum(z, 0.0) + jnp.log1p(jnp.exp(-jnp.abs(z)))
    step = jnp.where(lane < 2 * H, soft * keep_column(nb_ref), 0.0)
    fall = -step * prm_ref[1:2, :]
    row = iota((T, T), 0)
    col = iota((T, T), 1)
    c = jnp.where(
        lane < H,
        exact_left(ones_where(row >= col), fall),
        exact_left(ones_where(row <= col), fall),
    )
    last = jnp.where(lane[0:1] < H, c[T - 1 : T], c[0:1])
    a = jnp.where(step > 0.0, jnp.log(jnp.maximum(step, 1e-37)) - c, FAR)
    z_ref[...] = z
    step_ref[...] = step
    c_ref[...] = c
    at_ref[...] = a.T
    bcf = proj[:, 128:256]
    bcr = proj[:, 256:384]
    bcf_ref[...] = bcf
    bcr_ref[...] = bcr

    e2 = jnp.concatenate(split2(jnp.exp(c)), axis=1)
    tail2 = jnp.concatenate(split2(jnp.exp(last - c) * step), axis=1)
    decay = jnp.exp(last)
    decay8 = jnp.broadcast_to(decay, (8, 128))
    tf_hi, tf_lo = split2(bcf.T)
    tr_hi, tr_lo = split2(bcr.T)
    both = [
        jnp.concatenate([hi[s], lo[s]], axis=0)
        for hi, lo, s in (
            (tf_hi, tf_lo, slice(0, N)),
            (tr_hi, tr_lo, slice(N, 2 * N)),
            (tr_hi, tr_lo, slice(0, N)),
            (tf_hi, tf_lo, slice(N, 2 * N)),
        )
    ]

    def states(j, carry):
        cols = pl.ds(pl.multiple_of(j * 128, 128), 128)
        sel = spread(j, 128)
        sel2 = jnp.concatenate([sel, sel], axis=0)
        ee = mat(e2, sel2)
        tt = mat(tail2, sel2)
        dd = exact_right(decay8, sel)
        xj = x_ref[:, cols].astype(F32)
        dj = dy_ref[:, cols].astype(F32)
        right = (tt[:, 0:128] * xj, ee[:, 128:256] * dj, tt[:, 128:256] * xj, ee[:, 0:128] * dj)
        drop = (dd[:, 0:128], dd[:, 128:256], dd[:, 128:256], dd[:, 0:128])
        half = j // 8
        part = j % 8
        for s in range(4):
            hi, lo = split2(right[s])
            wide = mat(both[s], hi)
            pack_ref[half, s, part, 0:N, :] = wide[0:N] + wide[N : 2 * N] + mat(both[s][0:N], lo)
            pack_ref[half, s, part, N : N + 8, :] = drop[s]
        return carry

    lax.fori_loop(0, G, states, 0)


def carry_kernel(chips, pack_ref, out_ref, other, total, drop, came, stage, give,
                 sem_a, sem_b, sem_c, sem_d, sem_e, sem_f):
    dp = lax.axis_index("dp")
    ctx = lax.axis_index("ctx")
    core = ctx % 2
    chip = ctx // 2
    partner = (dp, ctx + 1 - 2 * core)
    after = (dp, jnp.minimum(ctx + 2, 2 * chips - 2 + core))
    before = (dp, jnp.maximum(ctx - 2, core))

    barrier = pltpu.get_barrier_semaphore()
    pl.semaphore_signal(barrier, inc=1, device_id=partner, device_id_type=MESH)

    @pl.when(chip < chips - 1)
    def _():
        pl.semaphore_signal(barrier, inc=1, device_id=after, device_id_type=MESH)

    @pl.when(chip > 0)
    def _():
        pl.semaphore_signal(barrier, inc=1, device_id=before, device_id_type=MESH)

    peers = 1 + (chip < chips - 1).astype(jnp.int32) + (chip > 0).astype(jnp.int32)
    pl.semaphore_wait(barrier, peers)

    def swap(s):
        return pltpu.make_async_remote_copy(
            src_ref=pack_ref.at[1 - core, s], dst_ref=other.at[s],
            send_sem=sem_a.at[s], recv_sem=sem_b.at[s],
            device_id=partner, device_id_type=MESH,
        )

    for s in range(4):
        swap(s).start()

    @pl.when(chip == 0)
    def _():
        came[0:16] = jnp.zeros((16, N, 128), F32)

    @pl.when(chip == chips - 1)
    def _():
        came[16:32] = jnp.zeros((16, N, 128), F32)

    for s in range(4):
        swap(s).wait_recv()
    for s in range(4):
        first = core == (0 if s < 2 else 1)

        def sums(g, carry, s=s, first=first):
            mine = pack_ref[core, s, g, 0:N, :]
            theirs = other[s, g, 0:N, :]
            dm = pack_ref[core, s, g, N : N + 1, :]
            dt = other[s, g, N : N + 1, :]
            total[8 * s + g] = jnp.where(first, dt * mine + theirs, dm * theirs + mine)
            drop[8 * s + g] = jnp.broadcast_to(dm * dt, (8, 128))
            return carry

        lax.fori_loop(0, 8, sums, 0)

    def hop(i, target):
        return pltpu.make_async_remote_copy(
            src_ref=stage.at[i], dst_ref=came.at[i],
            send_sem=sem_c.at[i], recv_sem=sem_d.at[i],
            device_id=target, device_id_type=MESH,
        )

    def hand(i):
        return pltpu.make_async_remote_copy(
            src_ref=give.at[i], dst_ref=out_ref.at[core, i // 8, i % 8],
            send_sem=sem_e.at[i], recv_sem=sem_f.at[i],
            device_id=partner, device_id_type=MESH,
        )

    def piece(i, has_prev, has_next, target, first):
        @pl.when(has_prev)
        def _():
            hop(i, target).wait_recv()

        got = came[i]

        @pl.when(has_next)
        def _():
            stage[i] = drop[i, 0:1, :] * got + total[i]
            hop(i, target).start()

        s = i // 8
        g = i % 8
        mine = pack_ref[core, s, g, 0:N, :]
        theirs = other[s, g, 0:N, :]
        dm = pack_ref[core, s, g, N : N + 1, :]
        dt = other[s, g, N : N + 1, :]
        out_ref[core, s, g] = jnp.where(first, got, dt * got + theirs)
        give[i] = jnp.where(first, dm * got + mine, got)
        hand(i).start()

    def turn(tau, carry):
        up = tau - RATIO * chip
        down = tau - RATIO * (chips - 1 - chip)

        @pl.when((up >= 0) & (up < 16))
        def _():
            piece(up, chip > 0, chip < chips - 1, after, core == 0)

        @pl.when((down >= 0) & (down < 16))
        def _():
            piece(16 + down, chip < chips - 1, chip > 0, before, core == 1)

        return carry

    lax.fori_loop(0, RATIO * (chips - 1) + 16, turn, 0)

    def finish(i, carry):
        pltpu.make_async_remote_copy(
            src_ref=give.at[i], dst_ref=out_ref.at[1 - core, i // 8, i % 8],
            send_sem=sem_e.at[i], recv_sem=sem_f.at[i],
            device_id=partner, device_id_type=MESH,
        ).wait_recv()
        hand(i).wait_send()
        return carry

    lax.fori_loop(0, 32, finish, 0)

    @pl.when(chip < chips - 1)
    def _():
        def sent(i, carry):
            hop(i, after).wait_send()
            return carry

        lax.fori_loop(0, 16, sent, 0)

    @pl.when(chip > 0)
    def _():
        def sent(i, carry):
            hop(i, before).wait_send()
            return carry

        lax.fori_loop(16, 32, sent, 0)

    for s in range(4):
        swap(s).wait_send()


def inner_setup(c_ref, bcf_ref, bcr_ref, sc, c3, dsc):
    bcf = bcf_ref[...]
    bcr = bcr_ref[...]
    row = iota((T, T), 0)
    col = iota((T, T), 1)
    sf = mat3_nt(bcf[:, N:], bcf[:, :N])
    sr = mat3_nt(bcr[:, N:], bcr[:, :N])
    sc[...] = jnp.where(row > col, sf, jnp.where(row < col, sr, 0.0))
    c3[...] = jnp.concatenate(split3(c_ref[...]), axis=1)
    dsc[...] = jnp.zeros((T, T), F32)


def inner_pair(i, x_ref, dy_ref, at_ref, sc, c3, y_ref, dx_ref, dsc, rs_ref, cs_ref):
    cols = pl.ds(pl.multiple_of(i * 128, 128), 128)
    xp = x_ref[:, cols]
    dp = dy_ref[:, cols]
    dpt = dp.astype(F32).T.astype(BF16)
    lane = iota((1, 128), 1)
    row = iota((BLOCK, BLOCK), 0)
    col = iota((BLOCK, BLOCK), 1)
    low = row > col
    up = row < col
    lanes = iota((T, 128), 1)
    y = jnp.zeros((T, 128), F32)
    dut = []
    for k in range(2):
        h = 2 * i + k
        mask = ones_where((lane // N) == k)
        xm = xp * mask
        cross = mat_nt(dp * mask, xp)
        rows3 = iota((384, T), 0) % 128
        cols3 = iota((384, T), 1)
        sel = ones_where(rows3 == h + jnp.where(cols3 < 128, 0, H))
        cb = mat(c3[...], sel)
        af = at_ref[pl.ds(h, 1), :]
        ar = at_ref[pl.ds(H + h, 1), :]
        top = slice(0, BLOCK)
        bot = slice(BLOCK, T)

        def args(rows, columns):
            forward = cb[rows, 0:128] + af[:, columns]
            reverse = cb[rows, 128:256] + ar[:, columns]
            return forward, reverse

        e = {}
        for r in (top, bot):
            for q in (top, bot):
                f, b = args(r, q)
                if r is q:
                    arg = jnp.where(low, f, jnp.where(up, b, FAR))
                else:
                    arg = f if r is bot else b
                e[r is bot, q is bot] = jnp.exp(arg)
        kk = {}
        g = {}
        for r in (top, bot):
            for q in (top, bot):
                key = (r is bot, q is bot)
                kk[key] = sc[r, q] * e[key]
                xx = cross[r, q]
                g[key] = xx * kk[key]
                dsc[r, q] += xx * e[key]
        g0f = jnp.where(low, g[False, False], 0.0)
        g0r = g[False, False] - g0f
        g1f = jnp.where(low, g[True, True], 0.0)
        g1r = g[True, True] - g1f
        rf = jnp.concatenate(
            [jnp.sum(g0f, axis=1, keepdims=True),
             jnp.sum(g[True, False] + g1f, axis=1, keepdims=True)], axis=0)
        rr = jnp.concatenate(
            [jnp.sum(g0r + g[False, True], axis=1, keepdims=True),
             jnp.sum(g1r, axis=1, keepdims=True)], axis=0)
        rs_ref[...] = jnp.where(lanes == h, rf, jnp.where(lanes == H + h, rr, rs_ref[...]))
        cs_ref[pl.ds(h, 1), :] = jnp.concatenate(
            [jnp.sum(g0f + g[True, False], axis=0, keepdims=True),
             jnp.sum(g1f, axis=0, keepdims=True)], axis=1)
        cs_ref[pl.ds(H + h, 1), :] = jnp.concatenate(
            [jnp.sum(g0r, axis=0, keepdims=True),
             jnp.sum(g[False, True] + g1r, axis=0, keepdims=True)], axis=1)
        full = jnp.concatenate(
            [jnp.concatenate([kk[False, False], kk[False, True]], axis=1),
             jnp.concatenate([kk[True, False], kk[True, True]], axis=1)], axis=0)
        hi, lo = split2(full)
        y = y + mat(hi, xm) + mat(lo, xm)
        rows = dpt[N * k : N * (k + 1), :]
        dut.append(mat(rows, hi) + mat(rows, lo))
    y_ref[:, cols] = y
    dx_ref[:, cols] = jnp.concatenate(dut, axis=0).T


def inner_kernel(x_ref, dy_ref, c_ref, at_ref, bcf_ref, bcr_ref,
                 y_ref, dx_ref, dsc_ref, rs_ref, cs_ref, sc, c3):
    inner_setup(c_ref, bcf_ref, bcr_ref, sc, c3, dsc_ref)
    rs_ref[...] = jnp.zeros((T, 128), F32)
    cs_ref[...] = jnp.zeros((128, T), F32)

    def one(i, carry):
        inner_pair(i, x_ref, dy_ref, at_ref, sc, c3, y_ref, dx_ref, dsc_ref, rs_ref, cs_ref)
        return carry

    lax.fori_loop(0, G, one, 0)


def back_kernel(x_ref, dy_ref, nb_ref, prm_ref, c_ref, step_ref, z_ref, bcf_ref, bcr_ref,
                whi_ref, wlo_ref, yin_ref, dxin_ref, dsc_ref, rs_ref, cs_ref, car_ref,
                mixed_ref, dseq_ref, grad_ref,
                dx, rho, kap, xi, omega, dcf, dbf, dcr, dbr):
    lane = iota((T, 128), 1)
    c = c_ref[...]
    step = step_ref[...]
    z = z_ref[...]
    bcf = bcf_ref[...]
    bcr = bcr_ref[...]
    last = jnp.where(lane[0:1] < H, c[T - 1 : T], c[0:1])
    e2 = jnp.concatenate(split2(jnp.exp(c)), axis=1)
    tail2 = jnp.concatenate(split2(jnp.exp(last - c) * step), axis=1)
    sig_f = jnp.sum(bcf[:, :N] * bcf[:, N:], axis=1, keepdims=True)
    sig_r = jnp.sum(bcr[:, :N] * bcr[:, N:], axis=1, keepdims=True)
    sigma = jnp.where(lane < H, sig_f, jnp.where(lane < 2 * H, sig_r, 0.0))
    coef3 = jnp.concatenate(split3(sigma * step + prm_ref[2:3, :]), axis=1)
    for ref in (rho, kap, xi):
        ref[...] = jnp.zeros((T, 128), F32)
    omega[...] = jnp.zeros((8, 128), F32)
    for ref in (dcf, dbf, dcr, dbr):
        ref[...] = jnp.zeros((T, N), F32)
    cuts = {"bf": split2(bcf[:, :N]), "cf": split2(bcf[:, N:]),
            "br": split2(bcr[:, :N]), "cr": split2(bcr[:, N:])}

    def times(name, right):
        lh, ll = cuts[name]
        rh, rl = right
        return mat(lh, rh) + (mat(ll, rh) + mat(lh, rl))

    def times_nt(left, right):
        lh, ll = split2(left)
        rh, rl = right
        return mat_nt(lh, rh) + (mat_nt(ll, rh) + mat_nt(lh, rl))

    def group(j, carry):
        cols = pl.ds(pl.multiple_of(j * 128, 128), 128)
        half = j // 8
        part = j % 8
        state_f = car_ref[half, 0, part]
        adj_r = car_ref[half, 1, part]
        state_r = car_ref[half, 2, part]
        adj_f = car_ref[half, 3, part]
        sel = spread(j, 128)
        sel2 = jnp.concatenate([sel, sel], axis=0)
        ee = mat(e2, sel2)
        tt = mat(tail2, sel2)
        one = sel[:, 0:128] + sel[:, 128:256]
        coef = mat(coef3, jnp.concatenate([one, one, one], axis=0))
        xj = x_ref[:, cols].astype(F32)
        dj = dy_ref[:, cols].astype(F32)
        sf2, sr2, af2, ar2 = split2(state_f), split2(state_r), split2(adj_f), split2(adj_r)
        ef, er = ee[:, 0:128], ee[:, 128:256]
        wf, wr = tt[:, 0:128] * xj, tt[:, 128:256] * xj
        yf = ef * times("cf", sf2)
        yr = er * times("cr", sr2)
        vf = times("bf", af2)
        vr = times("br", ar2)
        mixed_ref[:, cols] = (yin_ref[:, cols] + (yf + yr) + coef * xj).astype(BF16)
        dx[:, cols] = (
            dxin_ref[:, cols] + (tt[:, 0:128] * vf + tt[:, 128:256] * vr) + coef * dj
        )
        back = sel.astype(F32).T.astype(BF16)
        rho[...] += mat2(jnp.concatenate([dj * yf, dj * yr], axis=1), back)
        kap[...] += mat2(jnp.concatenate([wf * vf, wr * vr], axis=1), back)
        xi[...] += mat2(dj * xj, back[0:128] + back[128:256])
        inner = jnp.concatenate(
            [jnp.sum(state_f * adj_f, axis=0, keepdims=True),
             jnp.sum(state_r * adj_r, axis=0, keepdims=True)], axis=1)
        omega[...] += exact_right(jnp.broadcast_to(inner, (8, 256)), back)
        dcf[...] += times_nt(ef * dj, sf2)
        dcr[...] += times_nt(er * dj, sr2)
        dbf[...] += times_nt(wf, af2)
        dbr[...] += times_nt(wr, ar2)
        return carry

    lax.fori_loop(0, G, group, 0)

    row = iota((T, T), 0)
    col = iota((T, T), 1)
    colsum = cs_ref[...].T
    kappa = kap[...]
    through = rs_ref[...] - colsum + rho[...]
    ahead = ones_where(row <= col)
    behind = ones_where(row >= col)
    strict_behind = ones_where(row > col)
    strict_ahead = ones_where(row < col)
    d_fall = jnp.where(
        lane < H,
        exact_left(ahead, through) + exact_left(strict_behind, kappa),
        exact_left(behind, through) + exact_left(strict_ahead, kappa),
    ) + omega[0:1, :] * jnp.exp(last)
    small = jnp.exp(-jnp.abs(z))
    soft = jnp.maximum(z, 0.0) + jnp.log1p(small)
    sigmoid = jnp.where(z >= 0.0, 1.0, small) / (1.0 + small)
    ratio = jnp.where(z < -30.0, 1.0, sigmoid / jnp.maximum(soft, 1e-30))
    ksi = xi[...]
    diag = step * ksi
    straight = colsum + kappa + sigma * diag
    dz = straight * ratio - prm_ref[1:2, :] * d_fall * sigmoid * keep_column(nb_ref)
    dz = jnp.where(lane < 2 * H, dz, 0.0)

    ds_f = jnp.sum(jnp.where(lane < H, diag, 0.0), axis=1, keepdims=True)
    ds_r = jnp.sum(jnp.where((lane >= H) & (lane < 2 * H), diag, 0.0), axis=1, keepdims=True)
    dsc = dsc_ref[...]
    turned = dsc.T
    eq = row == col
    m_f = jnp.where(eq, ds_f, jnp.where(row > col, dsc, 0.0))
    m_r = jnp.where(eq, ds_r, jnp.where(row < col, dsc, 0.0))
    mt_f = jnp.where(eq, ds_f, jnp.where(row < col, turned, 0.0))
    mt_r = jnp.where(eq, ds_r, jnp.where(row > col, turned, 0.0))
    d_cf = dcf[...] + mat3(m_f, bcf[:, :N])
    d_bf = dbf[...] + mat3(mt_f, bcf[:, N:])
    d_cr = dcr[...] + mat3(m_r, bcr[:, :N])
    d_br = dbr[...] + mat3(mt_r, bcr[:, N:])
    dproj = jnp.concatenate([dz, d_bf, d_cf, d_br, d_cr], axis=1)
    p_hi, p_lo = split2(dproj)
    p_cat = jnp.concatenate([p_hi, p_lo, p_hi], axis=1)

    r128 = iota((128, 128), 0)
    c128 = iota((128, 128), 1)
    fold = ones_where(((r128 < H) & (r128 == c128))
                      | ((r128 >= H) & (r128 < 2 * H) & (r128 + c128 == 2 * H - 1)))
    vectors = jnp.concatenate(
        [jnp.sum(dz, axis=0, keepdims=True),
         -jnp.sum(step * d_fall, axis=0, keepdims=True),
         jnp.sum(ksi, axis=0, keepdims=True),
         jnp.zeros((5, 128), F32)], axis=0)
    rows_all = grad_ref.shape[0]
    grad_ref[D + D // 4 : rows_all, :] = jnp.zeros((rows_all - D - D // 4, 128), F32)
    grad_ref[D + D // 4 : D + D // 4 + 8, :] = exact_right(vectors, fold)

    rep_f = ones_where((r128 < H) & (r128 == c128 % H))
    rep_r = ones_where((r128 >= H) & (r128 < 2 * H) & (2 * H - 1 - r128 == c128 % H))

    def right_side(part):
        dt_f = mat(part[:, 0:128], rep_f).astype(BF16)
        dt_r = mat(part[:, 0:128], rep_r).astype(BF16)
        return jnp.concatenate(
            [jnp.concatenate([part[:, 128:256], dt_f], axis=1),
             jnp.concatenate([part[:, 256:384], dt_r], axis=1)], axis=0)

    r_hi = right_side(p_hi)
    r_lo = right_side(p_lo)
    flip = flip_rows()

    def final(j, carry):
        cols = pl.ds(pl.multiple_of(j * 128, 128), 128)
        far = pl.ds(pl.multiple_of((G - 1 - j) * 128, 128), 128)
        w_hi = whi_ref[cols, :]
        w_cat = jnp.concatenate([w_hi, w_hi, wlo_ref[cols, :]], axis=1)
        dseq_ref[:, cols] = (dx[:, cols] + mat_nt(p_cat, w_cat)).astype(BF16)
        x_here = x_ref[:, cols].astype(F32).T.astype(BF16)
        x_far = x_ref[:, far].astype(F32).T.astype(BF16)
        left = jnp.concatenate([x_here, mat(flip, x_far).astype(BF16)], axis=1)
        grads = mat(left, r_hi) + mat(left, r_lo)
        grad_ref[cols, :] = grads[:, 0:128]
        spot = pl.ds(pl.multiple_of(D + (j % 4) * 128, 128), 128)
        mine = iota((128, 128), 1) // H == j // 4
        grad_ref[spot, :] = jnp.where(
            mine, grads[:, 128:256], jnp.where(j < 4, 0.0, grad_ref[spot, :]))
        return carry

    lax.fori_loop(0, G, final, 0)


def sum_kernel(halves, depth, g_ref, out_ref, from_core, held, from_plane, part, from_z, full,
               s_core, r_core, s_plane, r_plane, s_z, r_z, s_zg, r_zg, s_pg, r_pg, s_cg, r_cg):
    dp = lax.axis_index("dp")
    ctx = lax.axis_index("ctx")
    plane = g_ref.shape[0] // 2
    tiles = g_ref.shape[1]
    zt = from_z.shape[1]
    core = ctx % 2
    z = (ctx // 2) % depth
    me = dp * halves + ctx // (2 * depth)
    partner = (dp, ctx + 1 - 2 * core)

    def plane_device(k):
        return (k // halves, ((k % halves) * depth + z) * 2 + core)

    def z_device(j):
        return (dp, ((ctx // (2 * depth)) * depth + j) * 2 + core)

    def peer(i):
        return lax.rem(me + 1 + i, plane)

    def z_peer(i):
        return lax.rem(z + 1 + i, depth)

    def remote(src, dst, send, recv, device):
        return pltpu.make_async_remote_copy(
            src_ref=src, dst_ref=dst, send_sem=send, recv_sem=recv,
            device_id=device, device_id_type=MESH,
        )

    def loop(count, body):
        def step(i, carry):
            body(i)
            return carry

        lax.fori_loop(0, count, step, 0)

    barrier = pltpu.get_barrier_semaphore()
    pl.semaphore_signal(barrier, inc=1, device_id=partner, device_id_type=MESH)
    loop(plane - 1, lambda i: pl.semaphore_signal(
        barrier, inc=1, device_id=plane_device(peer(i)), device_id_type=MESH))
    loop(depth - 1, lambda i: pl.semaphore_signal(
        barrier, inc=1, device_id=z_device(z_peer(i)), device_id_type=MESH))
    pl.semaphore_wait(barrier, plane + depth - 1)

    def core_copy(k):
        return remote(g_ref.at[(1 - core) * plane + k], from_core.at[k],
                      s_core.at[k], r_core.at[k], partner)

    def plane_copy(k):
        return remote(held.at[k], from_plane.at[me], s_plane.at[k], r_plane.at[me],
                      plane_device(k))

    loop(plane, lambda i: core_copy(peer(i)).start())

    def add_core(i):
        k = peer(i)
        core_copy(k).wait_recv()
        held[k] = g_ref[core * plane + k] + from_core[k]

    def forward(i):
        add_core(i)
        plane_copy(peer(i)).start()

    loop(plane - 1, forward)
    add_core(plane - 1)
    part[...] = jnp.zeros(part.shape, F32)
    part[0:tiles] = held[me]

    def add_plane(i):
        k = lax.rem(me + plane - 1 - i, plane)
        remote(held.at[k], from_plane.at[k], s_plane.at[k], r_plane.at[k],
               plane_device(k)).wait_recv()
        part[0:tiles] += from_plane[k]

    loop(plane - 1, add_plane)

    def z_copy(j):
        return remote(part.at[pl.ds(j * zt, zt)], from_z.at[z], s_z.at[j], r_z.at[z], z_device(j))

    loop(depth - 1, lambda i: z_copy(z_peer(i)).start())
    full[pl.ds(z * zt, zt)] = part[pl.ds(z * zt, zt)]

    def add_z(i):
        j = z_peer(i)
        remote(part.at[pl.ds(j * zt, zt)], from_z.at[j], s_z.at[j], r_z.at[j],
               z_device(j)).wait_recv()
        full[pl.ds(z * zt, zt)] += from_z[j]

    loop(depth - 1, add_z)

    def z_share(j):
        return remote(full.at[pl.ds(z * zt, zt)], full.at[pl.ds(z * zt, zt)],
                      s_zg.at[j], r_zg.at[z], z_device(j))

    loop(depth - 1, lambda i: z_share(z_peer(i)).start())

    def z_got(i):
        j = z_peer(i)
        remote(full.at[pl.ds(j * zt, zt)], full.at[pl.ds(j * zt, zt)],
               s_zg.at[j], r_zg.at[j], z_device(j)).wait_recv()

    loop(depth - 1, z_got)
    mine = core * plane + me
    out_ref[mine] = full[0:tiles]

    def plane_share(k):
        return remote(out_ref.at[mine], out_ref.at[mine], s_pg.at[k], r_pg.at[me], plane_device(k))

    def core_share(k):
        return remote(out_ref.at[core * plane + k], out_ref.at[core * plane + k],
                      s_cg.at[k], r_cg.at[k], partner)

    loop(plane - 1, lambda i: plane_share(peer(i)).start())
    core_share(me).start()

    def plane_got(i):
        k = lax.rem(me + plane - 1 - i, plane)
        spot = out_ref.at[core * plane + k]
        remote(spot, spot, s_pg.at[k], r_pg.at[k], plane_device(k)).wait_recv()
        core_share(k).start()

    loop(plane - 1, plane_got)

    def core_got(k):
        spot = out_ref.at[(1 - core) * plane + k]
        remote(spot, spot, s_cg.at[k], r_cg.at[k], partner).wait_recv()

    loop(plane, core_got)
    loop(plane, lambda k: core_copy(k).wait_send())
    loop(plane, lambda k: core_share(k).wait_send())
    loop(plane - 1, lambda i: plane_copy(peer(i)).wait_send())
    loop(plane - 1, lambda i: plane_share(peer(i)).wait_send())
    loop(depth - 1, lambda i: z_copy(z_peer(i)).wait_send())
    loop(depth - 1, lambda i: z_share(z_peer(i)).wait_send())


def sds(shape, dtype=F32):
    return jax.ShapeDtypeStruct(shape, dtype)


def local_call(kernel, ins, outs, scratch=()):
    return pl.pallas_call(
        kernel,
        out_shape=outs,
        in_specs=ins,
        out_specs=[VMEM] * len(outs),
        scratch_shapes=list(scratch),
        compiler_params=pltpu.CompilerParams(vmem_limit_bytes=LIMIT),
    )


def on_device(sizes, sequence, n_blocks, w_dt, dt_bias, decay_rate, w_b, w_c, d_skip, cotangent):
    dps, ctxs = sizes
    halves = 2 if ctxs % 4 == 0 else 1
    depth = ctxs // (2 * halves)
    plane = dps * halves
    tiles = -(-((D + D // 4) // 8 + 1) // (2 * plane))
    zt = -(-tiles // depth)
    x = sequence[0]
    dy = cotangent[0]
    prm = jnp.stack([dt_bias, decay_rate, d_skip])
    prm = jnp.pad(jnp.concatenate([prm, prm[:, ::-1]], axis=1), ((0, 5), (0, 64)))

    pack, c, step, z, at, bcf, bcr, whi, wlo = local_call(
        front_kernel,
        [VMEM, VMEM, SMEM, VMEM, VMEM, VMEM, VMEM],
        [sds((2, 4, 8, N + 8, 128)), sds((T, 128)), sds((T, 128)), sds((T, 128)),
         sds((128, T)), sds((T, 128)), sds((T, 128)), sds((D, 384), BF16), sds((D, 384), BF16)],
    )(x, dy, n_blocks, w_dt, w_b, w_c, prm)

    yin, dxin, dsc, rs, cs = local_call(
        inner_kernel,
        [VMEM] * 6,
        [sds((T, D)), sds((T, D)), sds((T, T)), sds((T, 128)), sds((128, T))],
        [pltpu.VMEM((T, T), F32), pltpu.VMEM((T, 384), BF16)],
    )(x, dy, c, at, bcf, bcr)

    dma = pltpu.SemaphoreType.DMA
    carried = pl.pallas_call(
        functools.partial(carry_kernel, ctxs // 2),
        out_shape=sds((2, 4, 8, N, 128)),
        in_specs=[VMEM],
        out_specs=VMEM,
        scratch_shapes=[
            pltpu.VMEM((4, 8, N + 8, 128), F32),
            pltpu.VMEM((32, N, 128), F32),
            pltpu.VMEM((32, 8, 128), F32),
            pltpu.VMEM((32, N, 128), F32),
            pltpu.VMEM((32, N, 128), F32),
            pltpu.VMEM((32, N, 128), F32),
            dma((4,)), dma((4,)), dma((32,)), dma((32,)), dma((32,)), dma((32,)),
        ],
        compiler_params=pltpu.CompilerParams(
            vmem_limit_bytes=LIMIT, collective_id=0, has_side_effects=True),
    )(pack)

    mixed, dseq, grads = local_call(
        back_kernel,
        [VMEM, VMEM, SMEM] + [VMEM] * 14,
        [sds((T, D), BF16), sds((T, D), BF16), sds((2 * plane * tiles * 8, 128))],
        [pltpu.VMEM((T, D), F32)] + [pltpu.VMEM((T, 128), F32)] * 3
        + [pltpu.VMEM((8, 128), F32)] + [pltpu.VMEM((T, N), F32)] * 4,
    )(x, dy, n_blocks, prm, c, step, z, bcf, bcr, whi, wlo, yin, dxin, dsc, rs, cs, carried)

    summed = pl.pallas_call(
        functools.partial(sum_kernel, halves, depth),
        out_shape=sds((2 * plane, tiles, 8, 128)),
        in_specs=[VMEM],
        out_specs=VMEM,
        scratch_shapes=[
            pltpu.VMEM((plane, tiles, 8, 128), F32),
            pltpu.VMEM((plane, tiles, 8, 128), F32),
            pltpu.VMEM((plane, tiles, 8, 128), F32),
            pltpu.VMEM((depth * zt, 8, 128), F32),
            pltpu.VMEM((depth, zt, 8, 128), F32),
            pltpu.VMEM((depth * zt, 8, 128), F32),
            dma((plane,)), dma((plane,)), dma((plane,)), dma((plane,)),
            dma((depth,)), dma((depth,)), dma((depth,)), dma((depth,)),
            dma((plane,)), dma((plane,)), dma((plane,)), dma((plane,)),
        ],
        compiler_params=pltpu.CompilerParams(
            vmem_limit_bytes=LIMIT, collective_id=1, has_side_effects=True),
    )(grads.reshape(2 * plane, tiles, 8, 128)).reshape(-1, 128)

    quarter = D // 4
    grad_dt = jnp.concatenate(
        [summed[D : D + quarter, H * q : H * (q + 1)] for q in range(4)], axis=0)
    vectors = summed[D + quarter : D + quarter + 3, :H]
    return (mixed[None], dseq[None], grad_dt, vectors[0], vectors[1],
            summed[:D, :N], summed[:D, N:], vectors[2])


def solution(mesh):
    sizes = (mesh.shape["dp"], mesh.shape["ctx"])
    return jax.shard_map(
        functools.partial(on_device, sizes),
        mesh=mesh,
        in_specs=(
            P("dp", "ctx", None),
            P("dp", "ctx"),
            P(), P(), P(), P(), P(), P(),
            P("dp", "ctx", None),
        ),
        out_specs=(P("dp", "ctx", None), P("dp", "ctx", None), P(), P(), P(), P(), P(), P()),
        check_vma=False,
    )
```

time: 1340 us -> 206 us (0.15); the launches traced: 1320 us -> 206 us
  local copies, waits for them, and re-layouts: 407 us -> 16.8 us
  other arithmetic: 276 us -> 2.19 us
  waiting for transfers between devices: 263 us -> 0 us
  matrix products: 189 us -> 0 us
  Pallas kernels: 0 us -> 186 us
  blocking collectives: 163 us -> 0 us
  between operations: 15.4 us -> 0.71 us
    dot_general x72 -> x0, matrix products: 189 us -> none  [the longest x12 63.5 us: advance(): jnp.einsum('hts,shp->thp', mixing, u_k.reshape(BLOCK, heads, head_size),...]
    pallas_call x0 -> x5, Pallas kernels: none -> 186 us  [the longest x1 80.4 us: on_device(): pl.pallas_call(functools.partial(carry_kernel, ctxs // 2), out_shape=sds(...]
    select_n x124 -> x0, other arithmetic: 183 us -> none  [turn(): jnp.where(position < mine, new, old)]
    psum x1 -> x0, waiting for transfers between devices: 170 us -> none  [on_device(): matrices, vectors = lax.psum((matrices, vectors), ('dp', 'ctx'))]
    dynamic_slice x158 -> x0, local copies, waits for them, and re-layouts: 123 us -> none  [the longest x124 79.9 us: turn(): longer = join(total, jax.tree.map(lambda part: part[position], pieces))]
    rev x9 -> x1, local copies, waits for them, and re-layouts: 99 us -> 0.09 us  [on_device(): prm[:, ::-1]]
    all_gather x4 -> x0, waiting for transfers between devices: 92.3 us -> none  [prefix(): pieces = jax.tree.map(lambda part: lax.all_gather(part, axis), value)]
    all_gather x2 -> x0, blocking collectives: 87.4 us -> none  [prefix(): pieces = jax.tree.map(lambda part: lax.all_gather(part, axis), value)]
  transfers between devices with their start and end apart: 5 -> 0, of which waited for: 3 -> 0; matrix products, arithmetic and copies ran while one was open for 29% -> 0% of each run, Pallas kernels for 0% -> 0%
where the time goes in v1:
time: 206 us
  Pallas kernels  186 us (90%)
  local copies, waits for them, and re-layouts  16.8 us (8%)
  other arithmetic  2.19 us (1%)
    pallas_call x1, Pallas kernels, on_device(): pl.pallas_call(functools.partial(carry_kernel, ctxs // 2), out_shape=sds(...  80.4 us
    pallas_call x1, Pallas kernels, on_device(): pl.pallas_call(functools.partial(sum_kernel, halves, depth), out_shape=sd...  40.2 us
    pallas_call x1, Pallas kernels, on_device(): local_call(back_kernel, [VMEM, VMEM, SMEM] + [VMEM] * 14, [sds((T, D), BF...  30 us
    pallas_call x1, Pallas kernels, on_device(): local_call(inner_kernel, [VMEM] * 6, [sds((T, D)), sds((T, D)), sds((T, T...  17.7 us
    pallas_call x1, Pallas kernels, on_device(): local_call(front_kernel, [VMEM, VMEM, SMEM, VMEM, VMEM, VMEM, VMEM], [sds...  17.5 us
    unnamed x25, local copies, waits for them, and re-layouts  15.5 us

profile of v1, /device:TPU:1, one launch (start us, length us, event | category | flops | bytes accessed | tf_op | source)
XLA Modules:
  0.0 205.6 jit_solution(17207613395122130848)
XLA Ops:
  0.6 0.7 pad_maximum_fusion.1
  1.3 0.1 rev.3
  1.4 0.8 select_maximum_fusion.prm_ref
  2.2 1.3 copy.17.wdt_ref
  3.5 0.0 copy-start
  3.5 0.0 copy-start.1
  3.5 0.0 copy-start.7
  3.5 2.5 %copy.18.wb_ref = f32[2048,64]{1,0:T(8,128)} copy(f32[2048,64]{0,1:T(8,128)} %param.14) | data formatting | bytes 1048576 | tf_op args[5]
  6.0 2.4 %copy.19.wc_ref = f32[2048,64]{1,0:T(8,128)} copy(f32[2048,64]{0,1:T(8,128)} %param.15) | data formatting | bytes 1048576 | tf_op args[6]
  8.4 0.0 copy-done
  8.4 0.0 copy-done.1
  8.4 0.0 copy-done.7
  8.4 0.0 copy-start.3
  8.4 1.2 copy-done.3
  9.6 0.0 copy-start.4
  9.6 1.2 copy-done.4
  10.8 17.5 %shard_map.152 = (f32[2,4,8,72,128]{4,3,2,1,0:T(8,128)}, f32[256,128]{1,0:T(8,128)S(1)}, f32[256,128]{1,0:T(8,128)S(1)}, f32[256,128]{1,0:T(8,128)S(1)}, f32[128...) custom-call(bf16[256,2048]{1,0:T(8,128)(2,1)S(1)} %bitcast.18, ...), custom_call_target="tpu_custom_call" | custom-call | tf_op jit(solution)/shard_map/pallas_call | solution.py:776
  28.3 0.0 copy-start.5
  28.3 1.7 copy-done.5
  30.0 80.4 %shard_map.154.car_ref = f32[2,4,8,64,128]{4,3,2,1,0:T(8,128)S(1)} custom-call(f32[2,4,8,72,128]{4,3,2,1,0:T(8,128)S(1)} %copy-done.5), custom_call_target="tpu_custom_call" | custom-call | tf_op jit(solution)/shard_map/pallas_call | solution.py:791
  110.4 0.0 copy-start.2
  110.4 1.3 copy-done.2
  111.7 17.7 %shard_map.153 = (f32[256,2048]{1,0:T(8,128)S(1)}, f32[256,2048]{1,0:T(8,128)}, f32[256,256]{1,0:T(8,128)S(1)}, f32[256,128]{1,0:T(8,128)S(1)}, f32[128,256]{1,0:T(8,128)S(1)}) custom-call(bf16[256,2048]{1,0:T(8,128)(2,1)S(1)} %bitcast.19, bf16[256,2048]{1,0:T(8,128)(2,1)S(1)} %bitcast.22, f32[256,128]{1,0:T(8,128)S(1)} %get-tuple-element.25.c_ref, ...), custom_call_target="tpu_custom_call" | custom-call | tf_op jit(solution)/shard_map/pallas_call | solution.py:783
  129.5 0.0 copy-start.6
  129.5 1.3 copy-done.6
  130.8 30.0 %shard_map.155 = (bf16[256,2048]{1,0:T(8,128)(2,1)}, bf16[256,2048]{1,0:T(8,128)(2,1)}, f32[2816,128]{1,0:T(8,128)S(1)}) custom-call(bf16[256,2048]{1,0:T(8,128)(2,1)S(1)} %bitcast.20, bf16[256,2048]{1,0:T(8,128)(2,1)S(1)} %bitcast.23, s32[1,2]{1,0:T(1,128)S(1)} %copy-done.7, f32[8,128]{1,0:T(8,128)S(1)} %select_maximum_fusion.prm_ref, ...), custom_call_target="tpu_custom_call" | custom-call | tf_op jit(solution)/shard_map/pallas_call | solution.py:809
  160.8 40.2 %shard_map.156 = f32[32,11,8,128]{3,2,1,0:T(8,128)S(1)} custom-call(f32[32,11,8,128]{3,2,1,0:T(8,128)S(1)} %bitcast.24), custom_call_target="tpu_custom_call" | custom-call | tf_op jit(solution)/shard_map/pallas_call | solution.py:817
  201.0 0.5 slice_bitcast_fusion
  201.6 0.3 fusion.1
  201.8 0.1 copy.26
  201.9 0.1 copy.29
  202.0 0.1 copy.28
  202.2 0.1 copy.27
  202.3 0.7 pad_maximum_fusion
  203.0 0.3 fusion
  203.3 1.1 copy.31
  204.4 1.1 copy.30
Async XLA Ops:
  3.5 4.9 %copy-start = (bf16[1,256,2048]{2,1,0:T(8,128)(2,1)S(1)}, bf16[1,256,2048]{2,1,0:T(8,128)(2,1)}, u32[]{:S(2)}) copy-start(bf16[1,256,2048]{2,1,0:T(8,128)(2,1)} %param.9) | copy-start | bytes 3145732
  3.5 4.9 %copy-start.1 = (bf16[1,256,2048]{2,1,0:T(8,128)(2,1)S(1)}, bf16[1,256,2048]{2,1,0:T(8,128)(2,1)}, u32[]{:S(2)}) copy-start(bf16[1,256,2048]{2,1,0:T(8,128)(2,1)} %param.17) | copy-start | bytes 3145732
  3.5 4.9 %copy-start.7 = (s32[1,2]{1,0:T(1,128)S(1)}, s32[1,2]{1,0:T(1,128)}, u32[]{:S(2)}) copy-start(s32[1,2]{1,0:T(1,128)} %nb_ref.3) | copy-start | bytes 28
  8.4 1.2 copy-start.3
  9.6 1.2 copy-start.4
  28.3 1.7 copy-start.5
  110.4 1.3 copy-start.2
  129.5 1.3 copy-start.6

commit v2 on v1

v2 whole, which is shorter than its diff:
```python
import functools

import jax
import jax.numpy as jnp
from jax import lax
from jax.experimental import pallas as pl
from jax.experimental.pallas import tpu as pltpu
from jax.sharding import PartitionSpec as P

F32 = jnp.float32
BF16 = jnp.bfloat16
BLOCK = 128
T = 256
D = 2048
H = 32
N = 64
G = 16
W = D // 256
MESH = pl.DeviceIdType.MESH
VMEM = pl.BlockSpec(memory_space=pltpu.VMEM)
SMEM = pl.BlockSpec(memory_space=pltpu.SMEM)
LIMIT = 48 * 1024 * 1024
ALL = 62 * 1024 * 1024
PIECES = 16
ROWS = 4 * 32 + 8
FAR = -1e30


def iota(shape, axis):
    return lax.broadcasted_iota(jnp.int32, shape, axis)


def mat(a, b):
    return lax.dot_general(a, b, (((1,), (0,)), ((), ())), preferred_element_type=F32)


def mat_nt(a, b):
    return lax.dot_general(a, b, (((1,), (1,)), ((), ())), preferred_element_type=F32)


def split2(a):
    hi = a.astype(BF16)
    return hi, (a - hi.astype(F32)).astype(BF16)


def split3(a):
    hi = a.astype(BF16)
    rest = a - hi.astype(F32)
    mid = rest.astype(BF16)
    return hi, mid, (rest - mid.astype(F32)).astype(BF16)


def mat2(a, exact):
    hi, lo = split2(a)
    return mat(hi, exact) + mat(lo, exact)


def mat3(a, b):
    ah, al = split2(a)
    bh, bl = split2(b)
    return mat(ah, bh) + (mat(al, bh) + mat(ah, bl))


def mat3_nt(a, b):
    ah, al = split2(a)
    bh, bl = split2(b)
    return mat_nt(ah, bh) + (mat_nt(al, bh) + mat_nt(ah, bl))


def exact_left(zero_one, a):
    hi, mid, lo = split3(a)
    return mat(zero_one, hi) + (mat(zero_one, mid) + mat(zero_one, lo))


def exact_right(a, zero_one):
    hi, mid, lo = split3(a)
    return mat(hi, zero_one) + (mat(mid, zero_one) + mat(lo, zero_one))


def ones_where(condition):
    return jnp.where(condition, 1.0, 0.0).astype(BF16)


def backwards(size):
    return ones_where(iota((size, size), 0) + iota((size, size), 1) == size - 1)


def keep_column(nb_ref):
    first = 1.0 - nb_ref[0, 0].astype(F32)
    second = 1.0 - nb_ref[0, 1].astype(F32)
    return jnp.where(iota((T, 1), 0) < BLOCK, first, second)


def spread(first, second):
    rows = iota((128, 256), 0)
    cols = iota((128, 256), 1)
    head = jnp.where(cols < 128, 2 * first, 2 * second) + (cols % 128) // N
    return ones_where(rows == head), ones_where(rows == head + H)


def twice(a):
    return jnp.concatenate([a, a], axis=0)


def lanes2(a):
    return jnp.concatenate(split2(a), axis=1)


def front_kernel(x_ref, dy_ref, nb_ref, wdt_ref, wb_ref, wc_ref, bias_ref, rate_ref, skip_ref,
                 pack_ref, prm_ref, c_ref, step_ref, z_ref, at_ref, bcf_ref, bcr_ref,
                 whi_ref, wlo_ref):
    flip = backwards(256)
    rev = backwards(H)
    both = ones_where((iota((H, 128), 1) == iota((H, 128), 0))
                      | (iota((H, 128), 1) + iota((H, 128), 0) == 2 * H - 1))
    for n, ref in enumerate((bias_ref, rate_ref, skip_ref)):
        prm_ref[n : n + 1, :] = exact_right(jnp.broadcast_to(ref[...], (8, H)), both)[0:1]
    prm_ref[3:8, :] = jnp.zeros((5, 128), F32)

    def cut(i, carry):
        here = pl.ds(pl.multiple_of(i * 256, 256), 256)
        there = pl.ds(pl.multiple_of((W - 1 - i) * 256, 256), 256)
        raw = jnp.concatenate([wdt_ref[:, here], wb_ref[:, here], wc_ref[:, here]], axis=0)
        hi, lo = split2(raw)
        turned = mat(jnp.concatenate([hi, lo], axis=0), flip).astype(BF16)
        for ref, own, far in ((whi_ref, hi, turned[0:160]), (wlo_ref, lo, turned[160:320])):
            ref[0:H, here] = own[0:H]
            ref[128:256, here] = own[H:160]
            ref[H : 2 * H, there] = mat(rev, far[0:H]).astype(BF16)
            ref[256:384, there] = far[H:160]
            ref[2 * H : 128, here] = jnp.zeros((2 * H, 256), BF16)
        return carry

    lax.fori_loop(0, W, cut, 0, unroll=2)

    x = x_ref[...]
    proj = mat_nt(x, whi_ref[...]) + mat_nt(x, wlo_ref[...])
    lane = iota((T, 128), 1)
    z = proj[:, 0:128] + prm_ref[0:1, :]
    soft = jnp.maximum(z, 0.0) + jnp.log1p(jnp.exp(-jnp.abs(z)))
    step = jnp.where(lane < 2 * H, soft * keep_column(nb_ref), 0.0)
    fall = -step * prm_ref[1:2, :]
    row = iota((T, T), 0)
    col = iota((T, T), 1)
    c = jnp.where(
        lane < H,
        exact_left(ones_where(row >= col), fall),
        exact_left(ones_where(row <= col), fall),
    )
    last = jnp.where(lane[0:1] < H, c[T - 1 : T], c[0:1])
    a = jnp.where(step > 0.0, jnp.log(jnp.maximum(step, 1e-37)) - c, FAR)
    z_ref[...] = z
    step_ref[...] = step
    c_ref[...] = c
    at_ref[...] = a.T
    bcf = proj[:, 128:256]
    bcr = proj[:, 256:384]
    bcf_ref[...] = bcf
    bcr_ref[...] = bcr

    e2 = lanes2(jnp.exp(c))
    tail2 = lanes2(jnp.exp(last - c) * step)
    decay8 = jnp.broadcast_to(jnp.exp(last), (8, 128))
    tf_hi, tf_lo = split2(bcf.T)
    tr_hi, tr_lo = split2(bcr.T)
    lefts = [
        jnp.concatenate([hi[part], lo[part]], axis=0)
        for hi, lo, part in (
            (tf_hi, tf_lo, slice(0, N)),
            (tr_hi, tr_lo, slice(N, 2 * N)),
            (tr_hi, tr_lo, slice(0, N)),
            (tf_hi, tf_lo, slice(N, 2 * N)),
        )
    ]

    def states(i, carry):
        cols = pl.ds(pl.multiple_of(i * 256, 256), 256)
        sel_f, sel_r = spread(2 * i, 2 * i + 1)
        two_f, two_r = twice(sel_f), twice(sel_r)
        xj = x_ref[:, cols].astype(F32)
        dj = dy_ref[:, cols].astype(F32)
        rights = (mat(tail2, two_f) * xj, mat(e2, two_r) * dj,
                  mat(tail2, two_r) * xj, mat(e2, two_f) * dj)
        dd_f, dd_r = exact_right(decay8, sel_f), exact_right(decay8, sel_r)
        which = iota((8, 256), 0)
        drops = jnp.where((which == 0) | (which == 3), dd_f, dd_r)
        half = i // (W // 2)
        for s in range(4):
            hi, lo = split2(rights[s])
            wide = mat(lefts[s], hi)
            got = wide[0:N] + wide[N : 2 * N] + mat(lefts[s][0:N], lo)
            for g in range(2):
                for r in range(2):
                    piece = 4 * (i % (W // 2)) + 2 * g + r
                    pack_ref[half, piece, 32 * s : 32 * s + 32, :] = got[
                        32 * r : 32 * r + 32, 128 * g : 128 * g + 128]
                    if s == 0:
                        pack_ref[half, piece, 128:ROWS, :] = drops[:, 128 * g : 128 * g + 128]
        return carry

    lax.fori_loop(0, W, states, 0)


def inner_setup(c_ref, bcf_ref, bcr_ref, sc, c3, dsc):
    bcf = bcf_ref[...]
    bcr = bcr_ref[...]
    row = iota((T, T), 0)
    col = iota((T, T), 1)
    sf = mat3_nt(bcf[:, N:], bcf[:, :N])
    sr = mat3_nt(bcr[:, N:], bcr[:, :N])
    sc[...] = jnp.where(row > col, sf, jnp.where(row < col, sr, 0.0))
    c3[...] = jnp.concatenate(split3(c_ref[...]), axis=1)
    dsc[...] = jnp.zeros((T, T), F32)


def inner_pair(i, x_ref, dy_ref, at_ref, sc, c3, y_ref, dx_ref, dsc, rs_ref, cs_ref, xi_ref):
    cols = pl.ds(pl.multiple_of(i * 128, 128), 128)
    xp = x_ref[:, cols]
    dp = dy_ref[:, cols]
    dpt = dp.astype(F32).T.astype(BF16)
    seg_rows = iota((128, 128), 0) // N + 2 * i
    seg_cols = iota((128, 128), 1)
    seg = ones_where((seg_cols < 2 * H) & (seg_cols % H == seg_rows))
    xi_ref[...] += mat2(dp.astype(F32) * xp.astype(F32), seg)
    lane = iota((1, 128), 1)
    row = iota((BLOCK, BLOCK), 0)
    col = iota((BLOCK, BLOCK), 1)
    low = row > col
    up = row < col
    lanes = iota((T, 128), 1)
    y = jnp.zeros((T, 128), F32)
    dut = []
    for k in range(2):
        h = 2 * i + k
        mask = ones_where((lane // N) == k)
        xm = xp * mask
        cross = mat_nt(dp * mask, xp)
        rows3 = iota((384, T), 0) % 128
        cols3 = iota((384, T), 1)
        sel = ones_where(rows3 == h + jnp.where(cols3 < 128, 0, H))
        cb = mat(c3[...], sel)
        af = at_ref[pl.ds(h, 1), :]
        ar = at_ref[pl.ds(H + h, 1), :]
        top = slice(0, BLOCK)
        bot = slice(BLOCK, T)

        def args(rows, columns):
            forward = cb[rows, 0:128] + af[:, columns]
            reverse = cb[rows, 128:256] + ar[:, columns]
            return forward, reverse

        e = {}
        for r in (top, bot):
            for q in (top, bot):
                f, b = args(r, q)
                if r is q:
                    arg = jnp.where(low, f, jnp.where(up, b, FAR))
                else:
                    arg = f if r is bot else b
                e[r is bot, q is bot] = jnp.exp(arg)
        kk = {}
        g = {}
        for r in (top, bot):
            for q in (top, bot):
                key = (r is bot, q is bot)
                kk[key] = sc[r, q] * e[key]
                xx = cross[r, q]
                g[key] = xx * kk[key]
                dsc[r, q] += xx * e[key]
        g0f = jnp.where(low, g[False, False], 0.0)
        g0r = g[False, False] - g0f
        g1f = jnp.where(low, g[True, True], 0.0)
        g1r = g[True, True] - g1f
        rf = jnp.concatenate(
            [jnp.sum(g0f, axis=1, keepdims=True),
             jnp.sum(g[True, False] + g1f, axis=1, keepdims=True)], axis=0)
        rr = jnp.concatenate(
            [jnp.sum(g0r + g[False, True], axis=1, keepdims=True),
             jnp.sum(g1r, axis=1, keepdims=True)], axis=0)
        rs_ref[...] = jnp.where(lanes == h, rf, jnp.where(lanes == H + h, rr, rs_ref[...]))
        cs_ref[pl.ds(h, 1), :] = jnp.concatenate(
            [jnp.sum(g0f + g[True, False], axis=0, keepdims=True),
             jnp.sum(g1f, axis=0, keepdims=True)], axis=1)
        cs_ref[pl.ds(H + h, 1), :] = jnp.concatenate(
            [jnp.sum(g0r, axis=0, keepdims=True),
             jnp.sum(g[False, True] + g1r, axis=0, keepdims=True)], axis=1)
        full = jnp.concatenate(
            [jnp.concatenate([kk[False, False], kk[False, True]], axis=1),
             jnp.concatenate([kk[True, False], kk[True, True]], axis=1)], axis=0)
        hi, lo = split2(full)
        y = y + mat(hi, xm) + mat(lo, xm)
        rows = dpt[N * k : N * (k + 1), :]
        dut.append(mat(rows, hi) + mat(rows, lo))
    y_ref[:, cols] = y
    dx_ref[:, cols] = jnp.concatenate(dut, axis=0).T


def middle_kernel(chips, x_ref, dy_ref, nb_ref, prm_ref, c_ref, step_ref, z_ref, at_ref, bcf_ref,
                  bcr_ref, whi_ref, wlo_ref, pack_ref,
                  mixed_ref, dseq_ref, grad_ref,
                  y_in, dx, dsc, rs, cs, xi, sc, c3, rho, kap, omega, acc, accl,
                  other, sums, inbox, outbox, came, give, carried,
                  s_swap, r_swap, s_in, r_in, s_out, r_out, s_hand, r_hand):
    per = PIECES // chips
    dp = lax.axis_index("dp")
    ctx = lax.axis_index("ctx")
    core = ctx % 2
    me = ctx // 2
    partner = (dp, ctx + 1 - 2 * core)

    def chip_device(k):
        return (dp, 2 * k + core)

    def peer(i):
        return lax.rem(me + 1 + i, chips)

    def remote(src, dst, send, recv, device):
        return pltpu.make_async_remote_copy(
            src_ref=src, dst_ref=dst, send_sem=send, recv_sem=recv,
            device_id=device, device_id_type=MESH,
        )

    def loop(count, body):
        def step(i, carry):
            body(i)
            return carry

        lax.fori_loop(0, count, step, 0)

    barrier = pltpu.get_barrier_semaphore()
    pl.semaphore_signal(barrier, inc=1, device_id=partner, device_id_type=MESH)
    loop(chips - 1, lambda i: pl.semaphore_signal(
        barrier, inc=1, device_id=chip_device(peer(i)), device_id_type=MESH))
    pl.semaphore_wait(barrier, chips)

    def block(k):
        return pl.ds(k * per, per)

    def swap(k):
        return remote(pack_ref.at[1 - core, block(k)], other.at[block(k)],
                      s_swap.at[k], r_swap.at[k], partner)

    loop(chips, lambda i: swap(peer(i)).start())
    first = [core == 0, core == 0, core == 1, core == 1]

    def add_up(k, place):
        swap(k).wait_recv()

        def one(u):
            p = k * per + u
            dm = pack_ref[core, p, 128:ROWS, :]
            dt = other[p, 128:ROWS, :]
            for s in range(4):
                rows = slice(32 * s, 32 * s + 32)
                mine = pack_ref[core, p, rows, :]
                theirs = other[p, rows, :]
                place[u, rows, :] = jnp.where(
                    first[s], dt[s : s + 1] * mine + theirs, dm[s : s + 1] * theirs + mine)
            place[u, 128:ROWS, :] = dm * dt

        loop(per, one)

    def to_owner(k):
        return remote(sums.at[k], inbox.at[me], s_in.at[k], r_in.at[me], chip_device(k))

    def send_sum(i):
        k = peer(i)
        add_up(k, sums.at[k])
        to_owner(k).start()

    loop(chips - 1, send_sum)
    add_up(me, inbox.at[me])

    inner_setup(c_ref, bcf_ref, bcr_ref, sc, c3, dsc)
    rs[...] = jnp.zeros((T, 128), F32)
    cs[...] = jnp.zeros((128, T), F32)
    xi[...] = jnp.zeros((T, 128), F32)
    loop(G, lambda i: inner_pair(
        i, x_ref, dy_ref, at_ref, sc, c3, y_in, dx, dsc, rs, cs, xi))
    for ref in (rho, kap, omega, acc, accl):
        ref[...] = jnp.zeros(ref.shape, F32)

    def got_sum(i):
        k = peer(i)
        remote(sums.at[k], inbox.at[k], s_in.at[k], r_in.at[k], chip_device(k)).wait_recv()

    loop(chips - 1, got_sum)

    def scan(u):
        def up(c, run):
            outbox[c, u, 0:64, :] = run
            drop = inbox[c, u, 128:ROWS, :]
            return jnp.concatenate(
                [drop[0:1] * run[0:32], drop[1:2] * run[32:64]], axis=0) + inbox[c, u, 0:64, :]

        def down(i, run):
            c = chips - 1 - i
            outbox[c, u, 64:128, :] = run
            drop = inbox[c, u, 128:ROWS, :]
            return jnp.concatenate(
                [drop[2:3] * run[0:32], drop[3:4] * run[32:64]], axis=0) + inbox[c, u, 64:128, :]

        def both(i, runs):
            return up(i, runs[0]), down(i, runs[1])

        zero = jnp.zeros((64, 128), F32)
        lax.fori_loop(0, chips, both, (zero, zero))

    loop(per, scan)

    def to_chip(k):
        return remote(outbox.at[k], came.at[me], s_out.at[k], r_out.at[me], chip_device(k))

    loop(chips - 1, lambda i: to_chip(peer(i)).start())
    came[me] = outbox[me]

    lane = iota((T, 128), 1)
    c = c_ref[...]
    step = step_ref[...]
    bcf = bcf_ref[...]
    bcr = bcr_ref[...]
    last = jnp.where(lane[0:1] < H, c[T - 1 : T], c[0:1])
    e2 = lanes2(jnp.exp(c))
    tail2 = lanes2(jnp.exp(last - c) * step)
    sig_f = jnp.sum(bcf[:, :N] * bcf[:, N:], axis=1, keepdims=True)
    sig_r = jnp.sum(bcr[:, :N] * bcr[:, N:], axis=1, keepdims=True)
    sigma = jnp.where(lane < H, sig_f, jnp.where(lane < 2 * H, sig_r, 0.0))
    coef3 = jnp.concatenate(split3(sigma * step + prm_ref[2:3, :]), axis=1)

    def left3(a):
        hi, lo = split2(a)
        return jnp.concatenate([hi, lo, hi], axis=1)

    l_bf, l_cf = left3(bcf[:, :N]), left3(bcf[:, N:])
    l_br, l_cr = left3(bcr[:, :N]), left3(bcr[:, N:])

    def group_of(i):
        return lax.rem(me * per // 2 + i, 8)

    def hand(g):
        spot = pl.ds(2 * g, 2)
        return remote(give.at[spot], carried.at[core, spot], s_hand.at[g], r_hand.at[g], partner)

    def receive(i):
        g = group_of(i)
        for r in range(2):
            p = 2 * g + r
            k = p // per

            if per == 1 or r == 0:
                @pl.when((k != me) & (p % per == 0))
                def _():
                    remote(outbox.at[k], came.at[k], s_out.at[k], r_out.at[k],
                           chip_device(k)).wait_recv()

            dm = pack_ref[core, p, 128:ROWS, :]
            dt = other[p, 128:ROWS, :]
            for s in range(4):
                rows = slice(32 * s, 32 * s + 32)
                got = came[k, p % per, rows, :]
                mine = pack_ref[core, p, rows, :]
                theirs = other[p, rows, :]
                carried[core, p, rows, :] = jnp.where(first[s], got, dt[s : s + 1] * got + theirs)
                give[p, rows, :] = jnp.where(first[s], dm[s : s + 1] * got + mine, got)
        hand(g).start()

    def work(i):
        g = group_of(i)
        remote(give.at[pl.ds(2 * g, 2)], carried.at[1 - core, pl.ds(2 * g, 2)],
               s_hand.at[g], r_hand.at[g], partner).wait_recv()
        groups = (8 * core + g, 8 * (1 - core) + g)
        places = [pl.ds(pl.multiple_of(j * 128, 128), 128) for j in groups]

        def wide(ref):
            return jnp.concatenate([ref[:, p] for p in places], axis=1)

        def state(s):
            rows = slice(32 * s, 32 * s + 32)
            return jnp.concatenate(
                [jnp.concatenate([carried[h, 2 * g, rows, :], carried[h, 2 * g + 1, rows, :]], axis=0)
                 for h in (core, 1 - core)], axis=1)

        state_f, adj_r, state_r, adj_f = state(0), state(1), state(2), state(3)
        sel_f, sel_r = spread(*groups)
        two_f, two_r = twice(sel_f), twice(sel_r)
        ef, er = mat(e2, two_f), mat(e2, two_r)
        tf, tr = mat(tail2, two_f), mat(tail2, two_r)
        one = sel_f + sel_r
        coef = mat(coef3, jnp.concatenate([one, one, one], axis=0))
        xj = wide(x_ref).astype(F32)
        dj = wide(dy_ref).astype(F32)
        wf, wr = tf * xj, tr * xj
        cuts = [split2(a) for a in (state_f, state_r, adj_f, adj_r)]

        def times(left, cut):
            return mat(left, jnp.concatenate([cut[0], cut[0], cut[1]], axis=0))

        yf = ef * times(l_cf, cuts[0])
        yr = er * times(l_cr, cuts[1])
        vf = times(l_bf, cuts[2])
        vr = times(l_br, cuts[3])
        out = wide(y_in) + (yf + yr) + coef * xj
        more = wide(dx) + (tf * vf + tr * vr) + coef * dj
        for n, p in enumerate(places):
            mixed_ref[:, p] = out[:, 128 * n : 128 * n + 128].astype(BF16)
            dx[:, p] = more[:, 128 * n : 128 * n + 128]
        back_f = sel_f.astype(F32).T.astype(BF16)
        back_r = sel_r.astype(F32).T.astype(BF16)
        rho[...] += mat2(dj * yf, back_f) + mat2(dj * yr, back_r)
        kap[...] += mat2(wf * vf, back_f) + mat2(wr * vr, back_r)
        in_f = jnp.sum(state_f * adj_f, axis=0, keepdims=True)
        in_r = jnp.sum(state_r * adj_r, axis=0, keepdims=True)
        omega[...] += (exact_right(jnp.broadcast_to(in_f, (8, 256)), back_f)
                       + exact_right(jnp.broadcast_to(in_r, (8, 256)), back_r))
        for n, (left, cut) in enumerate(zip((ef * dj, er * dj, wf, wr), cuts)):
            hi, lo = split2(left)
            acc[n] += mat_nt(hi, jnp.concatenate(cut, axis=0))
            accl[n] += mat_nt(lo, cut[0])

    def arrive(i):
        @pl.when(i < 8)
        def _():
            receive(i)

        @pl.when(i > 0)
        def _():
            work(i - 1)

    loop(9, arrive)

    def total(n):
        a = acc[n]
        return a[:, :N] + a[:, N:] + accl[n]

    z = z_ref[...]
    row = iota((T, T), 0)
    col = iota((T, T), 1)
    colsum = cs[...].T
    kappa = kap[...]
    through = rs[...] - colsum + rho[...]
    d_fall = jnp.where(
        lane < H,
        exact_left(ones_where(row <= col), through) + exact_left(ones_where(row > col), kappa),
        exact_left(ones_where(row >= col), through) + exact_left(ones_where(row < col), kappa),
    ) + omega[0:1, :] * jnp.exp(last)
    small = jnp.exp(-jnp.abs(z))
    soft = jnp.maximum(z, 0.0) + jnp.log1p(small)
    sigmoid = jnp.where(z >= 0.0, 1.0, small) / (1.0 + small)
    ratio = jnp.where(z < -30.0, 1.0, sigmoid / jnp.maximum(soft, 1e-30))
    ksi = xi[...]
    diag = step * ksi
    straight = colsum + kappa + sigma * diag
    dz = straight * ratio - prm_ref[1:2, :] * d_fall * sigmoid * keep_column(nb_ref)
    dz = jnp.where(lane < 2 * H, dz, 0.0)

    ds_f = jnp.sum(jnp.where(lane < H, diag, 0.0), axis=1, keepdims=True)
    ds_r = jnp.sum(jnp.where((lane >= H) & (lane < 2 * H), diag, 0.0), axis=1, keepdims=True)
    mixing = dsc[...]
    turned = mixing.T
    eq = row == col
    m_f = jnp.where(eq, ds_f, jnp.where(row > col, mixing, 0.0))
    m_r = jnp.where(eq, ds_r, jnp.where(row < col, mixing, 0.0))
    mt_f = jnp.where(eq, ds_f, jnp.where(row < col, turned, 0.0))
    mt_r = jnp.where(eq, ds_r, jnp.where(row > col, turned, 0.0))
    d_bcf = jnp.concatenate([total(2) + mat3(mt_f, bcf[:, N:]), total(0) + mat3(m_f, bcf[:, :N])], axis=1)
    d_bcr = jnp.concatenate([total(3) + mat3(mt_r, bcr[:, N:]), total(1) + mat3(m_r, bcr[:, :N])], axis=1)
    dproj = jnp.concatenate([dz, d_bcf, d_bcr], axis=1)
    p_hi, p_lo = split2(dproj)
    p_cat = jnp.concatenate([p_hi, p_lo, p_hi], axis=1)

    r128 = iota((128, 128), 0)
    c128 = iota((128, 128), 1)
    fold = ones_where(((r128 < H) & (r128 == c128))
                      | ((r128 >= H) & (r128 < 2 * H) & (r128 + c128 == 2 * H - 1)))
    vectors = jnp.concatenate(
        [jnp.sum(dz, axis=0, keepdims=True),
         -jnp.sum(step * d_fall, axis=0, keepdims=True),
         jnp.sum(ksi, axis=0, keepdims=True),
         jnp.zeros((5, 128), F32)], axis=0)
    tiles_all = grad_ref.shape[0]
    grad_ref[20 * G : tiles_all] = jnp.zeros((tiles_all - 20 * G, 8, 128), F32)
    grad_ref[20 * G] = exact_right(vectors, fold)

    dz_t = dz.T
    f_t = jnp.concatenate([dz_t[0:H], d_bcf.T], axis=0)
    r_hi, r_lo = split2(jnp.concatenate([dz_t[H : 2 * H], d_bcr.T], axis=0))
    f_hi, f_lo = split2(f_t)
    rev = backwards(H)

    def ordered(a):
        return jnp.concatenate([mat(rev, a[0:H]).astype(BF16), a[H:]], axis=0)

    left = jnp.concatenate(
        [jnp.concatenate([f_hi, ordered(r_hi)], axis=1),
         jnp.concatenate([f_lo, ordered(r_lo)], axis=1)], axis=0)
    flip = backwards(256)

    def final(i):
        cols = pl.ds(pl.multiple_of(i * 256, 256), 256)
        far = pl.ds(pl.multiple_of((W - 1 - i) * 256, 256), 256)
        w_hi = whi_ref[:, cols]
        w_cat = jnp.concatenate([w_hi, w_hi, wlo_ref[:, cols]], axis=0)
        dseq_ref[:, cols] = (dx[:, cols] + mat(p_cat, w_cat)).astype(BF16)
        right = jnp.concatenate(
            [x_ref[:, cols], mat(x_ref[:, far], flip).astype(BF16)], axis=0)
        grads = mat(left, right)
        grads = grads[0:160] + grads[160:320]
        for r in range(20):
            for n in range(2):
                grad_ref[r * G + 2 * i + n] = grads[8 * r : 8 * r + 8, 128 * n : 128 * n + 128]

    loop(W, final)

    loop(chips, lambda k: swap(k).wait_send())
    loop(chips - 1, lambda i: to_owner(peer(i)).wait_send())
    loop(chips - 1, lambda i: to_chip(peer(i)).wait_send())
    loop(8, lambda g: hand(g).wait_send())


def sum_kernel(halves, depth, g_ref, dt_ref, b_ref, c_ref, vec_ref, out_ref, from_core, held, from_plane, part, from_z, full,
               s_core, r_core, s_plane, r_plane, s_z, r_z, s_zg, r_zg, s_pg, r_pg, s_cg, r_cg):
    dp = lax.axis_index("dp")
    ctx = lax.axis_index("ctx")
    plane = g_ref.shape[0] // 2
    tiles = g_ref.shape[1]
    zt = from_z.shape[1]
    core = ctx % 2
    z = (ctx // 2) % depth
    me = dp * halves + ctx // (2 * depth)
    partner = (dp, ctx + 1 - 2 * core)

    def plane_device(k):
        return (k // halves, ((k % halves) * depth + z) * 2 + core)

    def z_device(j):
        return (dp, ((ctx // (2 * depth)) * depth + j) * 2 + core)

    def peer(i):
        return lax.rem(me + 1 + i, plane)

    def z_peer(i):
        return lax.rem(z + 1 + i, depth)

    def remote(src, dst, send, recv, device):
        return pltpu.make_async_remote_copy(
            src_ref=src, dst_ref=dst, send_sem=send, recv_sem=recv,
            device_id=device, device_id_type=MESH,
        )

    def loop(count, body):
        def step(i, carry):
            body(i)
            return carry

        lax.fori_loop(0, count, step, 0)

    barrier = pltpu.get_barrier_semaphore()
    pl.semaphore_signal(barrier, inc=1, device_id=partner, device_id_type=MESH)
    loop(plane - 1, lambda i: pl.semaphore_signal(
        barrier, inc=1, device_id=plane_device(peer(i)), device_id_type=MESH))
    loop(depth - 1, lambda i: pl.semaphore_signal(
        barrier, inc=1, device_id=z_device(z_peer(i)), device_id_type=MESH))
    pl.semaphore_wait(barrier, plane + depth - 1)

    def core_copy(k):
        return remote(g_ref.at[(1 - core) * plane + k], from_core.at[k],
                      s_core.at[k], r_core.at[k], partner)

    def plane_copy(k):
        return remote(held.at[k], from_plane.at[me], s_plane.at[k], r_plane.at[me],
                      plane_device(k))

    loop(plane, lambda i: core_copy(peer(i)).start())

    def add_core(i):
        k = peer(i)
        core_copy(k).wait_recv()
        held[k] = g_ref[core * plane + k] + from_core[k]

    def forward(i):
        add_core(i)
        plane_copy(peer(i)).start()

    loop(plane - 1, forward)
    add_core(plane - 1)
    part[...] = jnp.zeros(part.shape, F32)
    part[0:tiles] = held[me]

    def add_plane(i):
        k = lax.rem(me + plane - 1 - i, plane)
        remote(held.at[k], from_plane.at[k], s_plane.at[k], r_plane.at[k],
               plane_device(k)).wait_recv()
        part[0:tiles] += from_plane[k]

    loop(plane - 1, add_plane)

    def z_copy(j):
        return remote(part.at[pl.ds(j * zt, zt)], from_z.at[z], s_z.at[j], r_z.at[z], z_device(j))

    loop(depth - 1, lambda i: z_copy(z_peer(i)).start())
    full[pl.ds(z * zt, zt)] = part[pl.ds(z * zt, zt)]

    def add_z(i):
        j = z_peer(i)
        remote(part.at[pl.ds(j * zt, zt)], from_z.at[j], s_z.at[j], r_z.at[j],
               z_device(j)).wait_recv()
        full[pl.ds(z * zt, zt)] += from_z[j]

    loop(depth - 1, add_z)

    def z_share(j):
        return remote(full.at[pl.ds(z * zt, zt)], full.at[pl.ds(z * zt, zt)],
                      s_zg.at[j], r_zg.at[z], z_device(j))

    loop(depth - 1, lambda i: z_share(z_peer(i)).start())

    def z_got(i):
        j = z_peer(i)
        remote(full.at[pl.ds(j * zt, zt)], full.at[pl.ds(j * zt, zt)],
               s_zg.at[j], r_zg.at[j], z_device(j)).wait_recv()

    loop(depth - 1, z_got)
    mine = core * plane + me
    out_ref[mine] = full[0:tiles]

    def plane_share(k):
        return remote(out_ref.at[mine], out_ref.at[mine], s_pg.at[k], r_pg.at[me], plane_device(k))

    def core_share(k):
        return remote(out_ref.at[core * plane + k], out_ref.at[core * plane + k],
                      s_cg.at[k], r_cg.at[k], partner)

    loop(plane - 1, lambda i: plane_share(peer(i)).start())
    core_share(me).start()

    def plane_got(i):
        k = lax.rem(me + plane - 1 - i, plane)
        spot = out_ref.at[core * plane + k]
        remote(spot, spot, s_pg.at[k], r_pg.at[k], plane_device(k)).wait_recv()
        core_share(k).start()

    loop(plane - 1, plane_got)

    def core_got(k):
        spot = out_ref.at[(1 - core) * plane + k]
        remote(spot, spot, s_cg.at[k], r_cg.at[k], partner).wait_recv()

    loop(plane, core_got)

    def unpack(j):
        cols = pl.ds(pl.multiple_of(j * 128, 128), 128)
        for r in range(20):
            ref, base = (dt_ref, 0) if r < 4 else (b_ref, 4) if r < 12 else (c_ref, 12)
            n = r * G + j
            ref[8 * (r - base) : 8 * (r - base) + 8, cols] = out_ref[n // tiles, n % tiles]

    loop(G, unpack)
    vec_ref[...] = out_ref[20 * G // tiles, 20 * G % tiles]
    loop(plane, lambda k: core_copy(k).wait_send())
    loop(plane, lambda k: core_share(k).wait_send())
    loop(plane - 1, lambda i: plane_copy(peer(i)).wait_send())
    loop(plane - 1, lambda i: plane_share(peer(i)).wait_send())
    loop(depth - 1, lambda i: z_copy(z_peer(i)).wait_send())
    loop(depth - 1, lambda i: z_share(z_peer(i)).wait_send())


def sds(shape, dtype=F32):
    return jax.ShapeDtypeStruct(shape, dtype)


def on_device(sizes, sequence, n_blocks, w_dt, dt_bias, decay_rate, w_b, w_c, d_skip, cotangent):
    dps, ctxs = sizes
    chips = ctxs // 2
    halves = 2 if ctxs % 4 == 0 else 1
    depth = chips // halves
    plane = dps * halves
    tiles = -(-(20 * G + 1) // (2 * plane))
    zt = -(-tiles // depth)
    per = PIECES // chips
    x = sequence[0]
    dy = cotangent[0]
    dma = pltpu.SemaphoreType.DMA
    vmem = pltpu.VMEM

    outs = [sds((2, PIECES, ROWS, 128)), sds((8, 128)), sds((T, 128)), sds((T, 128)), sds((T, 128)),
            sds((128, T)), sds((T, 128)), sds((T, 128)), sds((384, D), BF16), sds((384, D), BF16)]
    pack, prm, c, step, z, at, bcf, bcr, whi, wlo = pl.pallas_call(
        front_kernel,
        out_shape=outs,
        in_specs=[VMEM, VMEM, SMEM] + [VMEM] * 6,
        out_specs=[VMEM] * len(outs),
        compiler_params=pltpu.CompilerParams(vmem_limit_bytes=ALL),
    )(x, dy, n_blocks, w_dt.T, w_b.T, w_c.T, dt_bias[None], decay_rate[None], d_skip[None])

    block = (chips, per)
    mixed, dseq, grads = pl.pallas_call(
        functools.partial(middle_kernel, chips),
        out_shape=[sds((T, D), BF16), sds((T, D), BF16), sds((2 * plane * tiles, 8, 128))],
        in_specs=[VMEM, VMEM, SMEM] + [VMEM] * 10,
        out_specs=[VMEM] * 3,
        scratch_shapes=[
            vmem((T, D), F32), vmem((T, D), F32), vmem((T, T), F32), vmem((T, 128), F32),
            vmem((128, T), F32), vmem((T, 128), F32), vmem((T, T), F32), vmem((T, 384), BF16),
            vmem((T, 128), F32), vmem((T, 128), F32), vmem((8, 128), F32),
            vmem((4, T, 128), F32), vmem((4, T, N), F32),
            vmem((PIECES, ROWS, 128), F32), vmem(block + (ROWS, 128), F32),
            vmem(block + (ROWS, 128), F32), vmem(block + (128, 128), F32),
            vmem(block + (128, 128), F32), vmem((PIECES, 128, 128), F32),
            vmem((2, PIECES, 128, 128), F32),
        ] + [dma((chips,))] * 6 + [dma((8,))] * 2,
        compiler_params=pltpu.CompilerParams(
            vmem_limit_bytes=ALL, collective_id=0, has_side_effects=True),
    )(x, dy, n_blocks, prm, c, step, z, at, bcf, bcr, whi, wlo, pack)

    grad_dt, grad_b, grad_c, vectors = pl.pallas_call(
        functools.partial(sum_kernel, halves, depth),
        out_shape=[sds((H, D)), sds((N, D)), sds((N, D)), sds((8, 128))],
        in_specs=[VMEM],
        out_specs=[VMEM] * 4,
        scratch_shapes=[
            vmem((2 * plane, tiles, 8, 128), F32),
            vmem((plane, tiles, 8, 128), F32),
            vmem((plane, tiles, 8, 128), F32),
            vmem((plane, tiles, 8, 128), F32),
            vmem((depth * zt, 8, 128), F32),
            vmem((depth, zt, 8, 128), F32),
            vmem((depth * zt, 8, 128), F32),
        ] + [dma((plane,))] * 4 + [dma((depth,))] * 4 + [dma((plane,))] * 4,
        compiler_params=pltpu.CompilerParams(
            vmem_limit_bytes=LIMIT, collective_id=1, has_side_effects=True),
    )(grads.reshape(2 * plane, tiles, 8, 128))

    return (mixed[None], dseq[None], grad_dt.T, vectors[0, :H], vectors[1, :H],
            grad_b.T, grad_c.T, vectors[2, :H])


def solution(mesh):
    sizes = (mesh.shape["dp"], mesh.shape["ctx"])
    return jax.shard_map(
        functools.partial(on_device, sizes),
        mesh=mesh,
        in_specs=(
            P("dp", "ctx", None),
            P("dp", "ctx"),
            P(), P(), P(), P(), P(), P(),
            P("dp", "ctx", None),
        ),
        out_specs=(P("dp", "ctx", None), P("dp", "ctx", None), P(), P(), P(), P(), P(), P()),
        check_vma=False,
    )
```

time: 206 us -> 155 us (0.75)
  Pallas kernels: 186 us -> 147 us
  local copies, waits for them, and re-layouts: 16.8 us -> 7.44 us
  other arithmetic: 2.19 us -> 0 us
    pallas_call x5 -> x3, Pallas kernels: 186 us -> 147 us  [the longest x1 88.9 us: on_device(): pl.pallas_call(functools.partial(middle_kernel, chips), out_shape=[sds((T...]
    unnamed x25 -> x9, local copies, waits for them, and re-layouts: 15.5 us -> 6.92 us
where the time goes in v2:
time: 155 us
  Pallas kernels  147 us (95%)
  local copies, waits for them, and re-layouts  7.44 us (5%)
    pallas_call x1, Pallas kernels, on_device(): pl.pallas_call(functools.partial(middle_kernel, chips), out_shape=[sds((T...  88.9 us
    pallas_call x1, Pallas kernels, on_device(): pl.pallas_call(functools.partial(sum_kernel, halves, depth), out_shape=[s...  45.2 us
    pallas_call x1, Pallas kernels, on_device(): pl.pallas_call(front_kernel, out_shape=outs, in_specs=[VMEM, VMEM, SMEM]...  13 us
    unnamed x9, local copies, waits for them, and re-layouts  6.92 us

profile of v2, /device:TPU:1, one launch (start us, length us, event | category | flops | bytes accessed | tf_op | source)
XLA Modules:
  0.0 155.2 jit_solution(15606764766664834946)
XLA Ops:
  0.6 13.0 %shard_map.152 = (f32[2,16,136,128]{3,2,1,0:T(8,128)}, f32[8,128]{1,0:T(8,128)}, f32[256,128]{1,0:T(8,128)}, f32[256,128]{1,0:T(8,128)}, f32[256,128]{1,0:T(8,12...) custom-call(bf16[256,2048]{1,0:T(8,128)(2,1)} %bitcast.24, ...), custom_call_target="tpu_custom_call" | custom-call | tf_op jit(solution)/shard_map/pallas_call | solution.py:787
  13.7 88.9 %shard_map.153 = (bf16[256,2048]{1,0:T(8,128)(2,1)}, bf16[256,2048]{1,0:T(8,128)(2,1)}, f32[352,8,128]{2,1,0:T(8,128)}) custom-call(bf16[256,2048]{1,0:T(8,128)(2,1)} %bitcast.25, bf16[256,2048]{1,0:T(8,128)(2,1)} %bitcast.27, s32[1,2]{1,0:T(1,128)} %nb_ref.3, f32[8,128]{1,0:T(8,128)} %get-tuple-element.25.prm_ref, f32[256,128]{1,0:T(8,128)} %get-tuple-element.26.c_ref, ...), custom_call_target="tpu_custom_call" | custom-call | tf_op jit(solution)/shard_map/pallas_call | solution.py:796
  102.6 0.0 copy-start
  102.6 1.4 copy-done
  103.9 0.0 copy-start.1
  103.9 45.2 %shard_map.154 = (f32[32,2048]{1,0:T(8,128)S(1)}, f32[64,2048]{1,0:T(8,128)S(1)}, f32[64,2048]{1,0:T(8,128)S(1)}, f32[8,128]{1,0:T(8,128)S(1)}) custom-call(f32[32,11,8,128]{3,2,1,0:T(8,128)S(1)} %bitcast.20), custom_call_target="tpu_custom_call" | custom-call | tf_op jit(solution)/shard_map/pallas_call | solution.py:815
  149.1 0.5 slice_bitcast_fusion
  149.6 2.3 %copy.22 = bf16[1,256,2048]{2,1,0:T(8,128)(2,1)} copy(bf16[1,256,2048]{2,1,0:T(8,128)(2,1)} %bitcast.29) | data formatting | bytes 2097152
  151.9 0.0 copy-done.1
  151.9 1.0 copy.23
  152.9 0.7 copy.24
  153.6 0.8 copy.25
  154.4 0.8 copy.26
Async XLA Ops:
  102.6 1.4 copy-start
  103.9 48.0 %copy-start.1 = (bf16[256,2048]{1,0:T(8,128)(2,1)S(1)}, bf16[256,2048]{1,0:T(8,128)(2,1)}, u32[]{:S(2)}) copy-start(bf16[256,2048]{1,0:T(8,128)(2,1)} %get-tuple-element.36) | copy-start | bytes 3145732

commit v3 on v2

v3 whole, which is shorter than its diff:
```python
import functools

import jax
import jax.numpy as jnp
from jax import lax
from jax.experimental import pallas as pl
from jax.experimental.pallas import tpu as pltpu
from jax.sharding import PartitionSpec as P

F32 = jnp.float32
BF16 = jnp.bfloat16
BLOCK = 128
T = 256
D = 2048
H = 32
N = 64
G = 16
W = D // 256
MESH = pl.DeviceIdType.MESH
VMEM = pl.BlockSpec(memory_space=pltpu.VMEM)
SMEM = pl.BlockSpec(memory_space=pltpu.SMEM)
ALL = 62 * 1024 * 1024
PIECES = 16
ROWS = (72, 64)
TILES = 20
FAR = -1e30
EARLY = 12


def iota(shape, axis):
    return lax.broadcasted_iota(jnp.int32, shape, axis)


def mat(a, b):
    return lax.dot_general(a, b, (((1,), (0,)), ((), ())), preferred_element_type=F32)


def mat_nt(a, b):
    return lax.dot_general(a, b, (((1,), (1,)), ((), ())), preferred_element_type=F32)


def split2(a):
    hi = a.astype(BF16)
    return hi, (a - hi.astype(F32)).astype(BF16)


def split3(a):
    hi = a.astype(BF16)
    rest = a - hi.astype(F32)
    mid = rest.astype(BF16)
    return hi, mid, (rest - mid.astype(F32)).astype(BF16)


def mat2(a, exact):
    hi, lo = split2(a)
    return mat(hi, exact) + mat(lo, exact)


def mat3(a, b):
    ah, al = split2(a)
    bh, bl = split2(b)
    return mat(ah, bh) + (mat(al, bh) + mat(ah, bl))


def mat3_nt(a, b):
    ah, al = split2(a)
    bh, bl = split2(b)
    return mat_nt(ah, bh) + (mat_nt(al, bh) + mat_nt(ah, bl))


def exact_left(zero_one, a):
    hi, mid, lo = split3(a)
    return mat(zero_one, hi) + (mat(zero_one, mid) + mat(zero_one, lo))


def exact_right(a, zero_one):
    hi, mid, lo = split3(a)
    return mat(hi, zero_one) + (mat(mid, zero_one) + mat(lo, zero_one))


def ones_where(condition):
    return jnp.where(condition, 1.0, 0.0).astype(BF16)


def backwards(size):
    return ones_where(iota((size, size), 0) + iota((size, size), 1) == size - 1)


def keep_column(nb_ref):
    first = 1.0 - nb_ref[0, 0].astype(F32)
    second = 1.0 - nb_ref[0, 1].astype(F32)
    return jnp.where(iota((T, 1), 0) < BLOCK, first, second)


def spread(first, second):
    rows = iota((128, 256), 0)
    cols = iota((128, 256), 1)
    head = jnp.where(cols < 128, 2 * first, 2 * second) + (cols % 128) // N
    return ones_where(rows == head), ones_where(rows == head + H)


def twice(a):
    return jnp.concatenate([a, a], axis=0)


def lanes2(a):
    return jnp.concatenate(split2(a), axis=1)


def inner_setup(c, bcf, bcr, sc, c3, dsc):
    row = iota((T, T), 0)
    col = iota((T, T), 1)
    sf = mat3_nt(bcf[:, N:], bcf[:, :N])
    sr = mat3_nt(bcr[:, N:], bcr[:, :N])
    sc[...] = jnp.where(row > col, sf, jnp.where(row < col, sr, 0.0))
    c3[...] = jnp.concatenate(split3(c), axis=1)
    dsc[...] = jnp.zeros((T, T), F32)


def inner_pair(i, x_ref, dy_ref, at_ref, sc, c3, y_ref, dx_ref, dsc, rs_ref, cs_ref, xi_ref):
    cols = pl.ds(pl.multiple_of(i * 128, 128), 128)
    xp = x_ref[:, cols]
    dp = dy_ref[:, cols]
    dpt = dp.astype(F32).T.astype(BF16)
    seg_rows = iota((128, 128), 0) // N + 2 * i
    seg_cols = iota((128, 128), 1)
    seg = ones_where((seg_cols < 2 * H) & (seg_cols % H == seg_rows))
    xi_ref[...] += mat2(dp.astype(F32) * xp.astype(F32), seg)
    lane = iota((1, 128), 1)
    row = iota((BLOCK, BLOCK), 0)
    col = iota((BLOCK, BLOCK), 1)
    low = row > col
    up = row < col
    lanes = iota((T, 128), 1)
    y = jnp.zeros((T, 128), F32)
    dut = []
    for k in range(2):
        h = 2 * i + k
        mask = ones_where((lane // N) == k)
        xm = xp * mask
        cross = mat_nt(dp * mask, xp)
        rows3 = iota((384, T), 0) % 128
        cols3 = iota((384, T), 1)
        sel = ones_where(rows3 == h + jnp.where(cols3 < 128, 0, H))
        cb = mat(c3[...], sel)
        af = at_ref[pl.ds(h, 1), :]
        ar = at_ref[pl.ds(H + h, 1), :]
        top = slice(0, BLOCK)
        bot = slice(BLOCK, T)

        def args(rows, columns):
            forward = cb[rows, 0:128] + af[:, columns]
            reverse = cb[rows, 128:256] + ar[:, columns]
            return forward, reverse

        e = {}
        for r in (top, bot):
            for q in (top, bot):
                f, b = args(r, q)
                if r is q:
                    arg = jnp.where(low, f, jnp.where(up, b, FAR))
                else:
                    arg = f if r is bot else b
                e[r is bot, q is bot] = jnp.exp(arg)
        kk = {}
        g = {}
        for r in (top, bot):
            for q in (top, bot):
                key = (r is bot, q is bot)
                kk[key] = sc[r, q] * e[key]
                xx = cross[r, q]
                g[key] = xx * kk[key]
                dsc[r, q] += xx * e[key]
        g0f = jnp.where(low, g[False, False], 0.0)
        g0r = g[False, False] - g0f
        g1f = jnp.where(low, g[True, True], 0.0)
        g1r = g[True, True] - g1f
        rf = jnp.concatenate(
            [jnp.sum(g0f, axis=1, keepdims=True),
             jnp.sum(g[True, False] + g1f, axis=1, keepdims=True)], axis=0)
        rr = jnp.concatenate(
            [jnp.sum(g0r + g[False, True], axis=1, keepdims=True),
             jnp.sum(g1r, axis=1, keepdims=True)], axis=0)
        rs_ref[...] = jnp.where(lanes == h, rf, jnp.where(lanes == H + h, rr, rs_ref[...]))
        cs_ref[pl.ds(h, 1), :] = jnp.concatenate(
            [jnp.sum(g0f + g[True, False], axis=0, keepdims=True),
             jnp.sum(g1f, axis=0, keepdims=True)], axis=1)
        cs_ref[pl.ds(H + h, 1), :] = jnp.concatenate(
            [jnp.sum(g0r, axis=0, keepdims=True),
             jnp.sum(g[False, True] + g1r, axis=0, keepdims=True)], axis=1)
        full = jnp.concatenate(
            [jnp.concatenate([kk[False, False], kk[False, True]], axis=1),
             jnp.concatenate([kk[True, False], kk[True, True]], axis=1)], axis=0)
        hi, lo = split2(full)
        y = y + mat(hi, xm) + mat(lo, xm)
        rows = dpt[N * k : N * (k + 1), :]
        dut.append(mat(rows, hi) + mat(rows, lo))
    y_ref[:, cols] = y
    dx_ref[:, cols] = jnp.concatenate(dut, axis=0).T


def kernel(chips, halves, depth, x_ref, dy_ref, nb_ref, wdt_ref, wb_ref, wc_ref,
           bias_ref, rate_ref, skip_ref,
           mixed_ref, dseq_ref, dt_ref, b_ref, c_ref, vec_ref,
           whi, wlo, at_ref, y_in, dx, dsc, rs, cs, xi, sc, c3, rho, kap, omega, acc, accl,
           pack_up, pack_down, other_up, other_down, sums_up, sums_down, in_up, in_down,
           out_up, out_down, came_up, came_down, give, carried,
           grad, all_ref, from_core, held, from_plane, part, from_z, full,
           s_swap, r_swap, s_in, r_in, s_out, r_out, s_hand, r_hand,
           s_core, r_core, s_plane, r_plane, s_z, r_z, s_zg, r_zg, s_pg, r_pg, s_cg, r_cg):
    per = PIECES // chips
    pack, other = (pack_up, pack_down), (other_up, other_down)
    sums, inbox = (sums_up, sums_down), (in_up, in_down)
    outbox, came = (out_up, out_down), (came_up, came_down)
    plane = held.shape[0]
    tiles = held.shape[1]
    zt = from_z.shape[1]
    dp = lax.axis_index("dp")
    ctx = lax.axis_index("ctx")
    core = ctx % 2
    chip = ctx // 2
    z_me = chip % depth
    p_me = dp * halves + chip // depth
    partner = (dp, ctx + 1 - 2 * core)

    def chip_device(k):
        return (dp, 2 * k + core)

    def chip_peer(i):
        return lax.rem(chip + 1 + i, chips)

    def plane_device(k):
        return (k // halves, ((k % halves) * depth + z_me) * 2 + core)

    def plane_peer(i):
        return lax.rem(p_me + 1 + i, plane)

    def z_device(k):
        return (dp, ((chip // depth) * depth + k) * 2 + core)

    def z_peer(i):
        return lax.rem(z_me + 1 + i, depth)

    def remote(src, dst, send, recv, device):
        return pltpu.make_async_remote_copy(
            src_ref=src, dst_ref=dst, send_sem=send, recv_sem=recv,
            device_id=device, device_id_type=MESH,
        )

    def loop(count, body, start=0):
        def step(i, carry):
            body(i)
            return carry

        lax.fori_loop(start, count, step, 0)

    barrier = pltpu.get_barrier_semaphore()
    pl.semaphore_signal(barrier, inc=1, device_id=partner, device_id_type=MESH)
    loop(chips - 1, lambda i: pl.semaphore_signal(
        barrier, inc=1, device_id=chip_device(chip_peer(i)), device_id_type=MESH))
    loop(plane - 1, lambda i: pl.semaphore_signal(
        barrier, inc=1, device_id=plane_device(plane_peer(i)), device_id_type=MESH))

    flip = backwards(256)
    rev = backwards(H)
    both = ones_where((iota((H, 128), 1) == iota((H, 128), 0))
                      | (iota((H, 128), 1) + iota((H, 128), 0) == 2 * H - 1))
    bias, rate, skip = (
        exact_right(jnp.broadcast_to(ref[...], (8, H)), both)[0:1]
        for ref in (bias_ref, rate_ref, skip_ref)
    )

    def cut(i, carry):
        here = pl.ds(pl.multiple_of(i * 256, 256), 256)
        there = pl.ds(pl.multiple_of((W - 1 - i) * 256, 256), 256)
        raw = jnp.concatenate([wdt_ref[:, here], wb_ref[:, here], wc_ref[:, here]], axis=0)
        hi, lo = split2(raw)
        turned = mat(jnp.concatenate([hi, lo], axis=0), flip).astype(BF16)
        for ref, own, far in ((whi, hi, turned[0:160]), (wlo, lo, turned[160:320])):
            ref[0:H, here] = own[0:H]
            ref[128:256, here] = own[H:160]
            ref[H : 2 * H, there] = mat(rev, far[0:H]).astype(BF16)
            ref[256:384, there] = far[H:160]
            ref[2 * H : 128, here] = jnp.zeros((2 * H, 256), BF16)
        return carry

    lax.fori_loop(0, W, cut, 0, unroll=2)

    x = x_ref[...]
    proj = mat_nt(x, whi[...]) + mat_nt(x, wlo[...])
    lane = iota((T, 128), 1)
    row = iota((T, T), 0)
    col = iota((T, T), 1)
    keep = keep_column(nb_ref)
    z = proj[:, 0:128] + bias
    soft = jnp.maximum(z, 0.0) + jnp.log1p(jnp.exp(-jnp.abs(z)))
    step = jnp.where(lane < 2 * H, soft * keep, 0.0)
    fall = -step * rate
    c = jnp.where(
        lane < H,
        exact_left(ones_where(row >= col), fall),
        exact_left(ones_where(row <= col), fall),
    )
    last = jnp.where(lane[0:1] < H, c[T - 1 : T], c[0:1])
    at_ref[...] = jnp.where(step > 0.0, jnp.log(jnp.maximum(step, 1e-37)) - c, FAR).T
    bcf = proj[:, 128:256]
    bcr = proj[:, 256:384]
    e2 = lanes2(jnp.exp(c))
    tail2 = lanes2(jnp.exp(last - c) * step)
    decay8 = jnp.broadcast_to(jnp.exp(last), (8, 128))
    tf_hi, tf_lo = split2(bcf.T)
    tr_hi, tr_lo = split2(bcr.T)

    lefts = [
        jnp.concatenate([hi[span], lo[span]], axis=0)
        for hi, lo, span in (
            (tf_hi, tf_lo, slice(0, N)),
            (tr_hi, tr_lo, slice(N, 2 * N)),
            (tr_hi, tr_lo, slice(0, N)),
            (tf_hi, tf_lo, slice(N, 2 * N)),
        )
    ]
    first = (core == 0, core == 1)

    def block(i):
        return lax.rem(i + chip * per // 4, 4)

    def swap(r, q):
        spot = pl.ds(4 * q, 4)
        return remote(pack[r].at[1 - core, spot], other[r].at[spot],
                      s_swap.at[r, q], r_swap.at[r, q], partner)

    def to_owner(r, p):
        return remote(sums[r].at[p, pl.ds(0, ROWS[r])], in_piece(r, chip, p % per),
                      s_in.at[r, p], r_in.at[r, chip * per + p % per], chip_device(p // per))

    def in_piece(r, k, u):
        return inbox[r].at[k, u]

    def local_states(r, half, q):
        i = 4 * half + q
        cols = pl.ds(pl.multiple_of(i * 256, 256), 256)
        sel_f, sel_r = spread(2 * i, 2 * i + 1)
        two_f, two_r = twice(sel_f), twice(sel_r)
        xj = x_ref[:, cols].astype(F32)
        dj = dy_ref[:, cols].astype(F32)
        if r == 0:
            rights = mat(tail2, two_f) * xj, mat(e2, two_r) * dj
            drops = jnp.where(iota((8, 256), 0) == 0,
                              exact_right(decay8, sel_f), exact_right(decay8, sel_r))
        else:
            rights = mat(tail2, two_r) * xj, mat(e2, two_f) * dj
        for s in range(2):
            left = lefts[2 * r + s]
            hi, lo = split2(rights[s])
            wide = mat(left, hi)
            got = wide[0:N] + wide[N : 2 * N] + mat(left[0:N], lo)
            for g in range(2):
                lanes = slice(128 * g, 128 * g + 128)
                for h in range(2):
                    p = 4 * q + 2 * g + h
                    pack[r][half, p, 32 * s : 32 * s + 32, :] = got[32 * h : 32 * h + 32, lanes]
                    if r == 0 and s == 0:
                        pack[r][half, p, 64:72, :] = drops[:, lanes]

    def drop_rows(r, p):
        mine = pack_up[core, p, 64:72, :]
        theirs = other_up[p, 64:72, :]
        order = (0, 1) if r == 0 else (1, 0)
        return [(mine[n : n + 1], theirs[n : n + 1]) for n in order]

    def add_up(r, q):
        swap(r, q).wait_recv()
        for n in range(4):
            p = 4 * q + n
            own = p // per == chip
            drops = drop_rows(r, p)
            out = []
            for s in range(2):
                rows = slice(32 * s, 32 * s + 32)
                dm, dt = drops[s]
                mine = pack[r][core, p, rows, :]
                theirs = other[r][p, rows, :]
                out.append(jnp.where(first[r], dt * mine + theirs, dm * theirs + mine))
            if r == 0:
                out.append(pack_up[core, p, 64:72, :] * other_up[p, 64:72, :])
            whole = jnp.concatenate(out, axis=0)

            @pl.when(own)
            def _():
                inbox[r][chip, p % per] = whole

            @pl.when(jnp.logical_not(own))
            def _():
                sums[r][p] = whole
                to_owner(r, p).start()

    pl.semaphore_wait(barrier, plane + chips - 1)
    for r in range(2):
        def states(i, r=r):
            @pl.when(i < 4)
            def _():
                q = block(i)
                local_states(r, 1 - core, q)
                swap(r, q).start()
                local_states(r, core, q)

            @pl.when(i > 0)
            def _():
                add_up(r, block(i - 1))

        loop(5, states)

    inner_setup(c, bcf, bcr, sc, c3, dsc)
    rs[...] = jnp.zeros((T, 128), F32)
    cs[...] = jnp.zeros((128, T), F32)
    xi[...] = jnp.zeros((T, 128), F32)
    for ref in (rho, kap, omega, acc, accl):
        ref[...] = jnp.zeros(ref.shape, F32)

    def inner(i):
        inner_pair(i, x_ref, dy_ref, at_ref, sc, c3, y_in, dx, dsc, rs, cs, xi)

    def to_chip(r, k):
        return remote(outbox[r].at[k], came[r].at[chip],
                      s_out.at[r, k], r_out.at[r, chip], chip_device(k))

    def scan(r):
        def arrived(i):
            k = chip_peer(i)
            for u in range(per):
                remote(sums[r].at[k * per + u, pl.ds(0, ROWS[r])], in_piece(r, k, u),
                       s_in.at[r, k * per + u], r_in.at[r, k * per + u],
                       chip_device(k)).wait_recv()

        loop(chips - 1, arrived)

        def piece(u):
            def turn(i, run):
                k = i if r == 0 else chips - 1 - i
                outbox[r][k, u] = run
                drop = in_up[k, u, 64:72, :]
                one, two = (drop[0:1], drop[1:2]) if r == 0 else (drop[1:2], drop[0:1])
                return (jnp.concatenate([one * run[0:32], two * run[32:64]], axis=0)
                        + inbox[r][k, u, 0:64, :])

            lax.fori_loop(0, chips, turn, jnp.zeros((64, 128), F32))

        loop(per, piece)
        loop(chips - 1, lambda i: to_chip(r, chip_peer(i)).start())
        came[r][chip] = outbox[r][chip]

    loop(EARLY, inner)
    scan(0)
    loop(G, inner, EARLY)
    scan(1)

    sig_f = jnp.sum(bcf[:, :N] * bcf[:, N:], axis=1, keepdims=True)
    sig_r = jnp.sum(bcr[:, :N] * bcr[:, N:], axis=1, keepdims=True)
    sigma = jnp.where(lane < H, sig_f, jnp.where(lane < 2 * H, sig_r, 0.0))
    coef3 = jnp.concatenate(split3(sigma * step + skip), axis=1)

    def left3(a):
        hi, lo = split2(a)
        return jnp.concatenate([hi, lo, hi], axis=1)

    l_bf, l_cf = left3(bcf[:, :N]), left3(bcf[:, N:])
    l_br, l_cr = left3(bcr[:, :N]), left3(bcr[:, N:])

    def group_of(i):
        return lax.rem(chip * per // 2 + i, 8)

    def hand(g):
        spot = pl.ds(2 * g, 2)
        return remote(give.at[spot], carried.at[core, spot], s_hand.at[g], r_hand.at[g], partner)

    def receive(i):
        g = group_of(i)
        for n in range(2):
            p = 2 * g + n
            k = p // per
            for r in range(2):
                @pl.when((k != chip) & (p % per == 0))
                def _():
                    remote(outbox[r].at[k], came[r].at[k], s_out.at[r, k], r_out.at[r, k],
                           chip_device(k)).wait_recv()

                drops = drop_rows(r, p)
                for s in range(2):
                    rows = slice(32 * s, 32 * s + 32)
                    to = slice(64 * r + 32 * s, 64 * r + 32 * s + 32)
                    dm, dt = drops[s]
                    got = came[r][k, p % per, rows, :]
                    mine = pack[r][core, p, rows, :]
                    theirs = other[r][p, rows, :]
                    carried[core, p, to, :] = jnp.where(first[r], got, dt * got + theirs)
                    give[p, to, :] = jnp.where(first[r], dm * got + mine, got)
        hand(g).start()

    def work(i):
        g = group_of(i)
        remote(give.at[pl.ds(2 * g, 2)], carried.at[1 - core, pl.ds(2 * g, 2)],
               s_hand.at[g], r_hand.at[g], partner).wait_recv()
        groups = (8 * core + g, 8 * (1 - core) + g)
        places = [pl.ds(pl.multiple_of(j * 128, 128), 128) for j in groups]

        def wide(ref):
            return jnp.concatenate([ref[:, p] for p in places], axis=1)

        def state(s):
            rows = slice(32 * s, 32 * s + 32)
            return jnp.concatenate(
                [jnp.concatenate([carried[h, 2 * g, rows, :], carried[h, 2 * g + 1, rows, :]], axis=0)
                 for h in (core, 1 - core)], axis=1)

        state_f, adj_r, state_r, adj_f = state(0), state(1), state(2), state(3)
        sel_f, sel_r = spread(*groups)
        two_f, two_r = twice(sel_f), twice(sel_r)
        ef, er = mat(e2, two_f), mat(e2, two_r)
        tf, tr = mat(tail2, two_f), mat(tail2, two_r)
        one = sel_f + sel_r
        coef = mat(coef3, jnp.concatenate([one, one, one], axis=0))
        xj = wide(x_ref).astype(F32)
        dj = wide(dy_ref).astype(F32)
        wf, wr = tf * xj, tr * xj
        cuts = [split2(a) for a in (state_f, state_r, adj_f, adj_r)]

        def times(left, cut):
            return mat(left, jnp.concatenate([cut[0], cut[0], cut[1]], axis=0))

        yf = ef * times(l_cf, cuts[0])
        yr = er * times(l_cr, cuts[1])
        vf = times(l_bf, cuts[2])
        vr = times(l_br, cuts[3])
        out = wide(y_in) + (yf + yr) + coef * xj
        more = wide(dx) + (tf * vf + tr * vr) + coef * dj
        for n, p in enumerate(places):
            mixed_ref[:, p] = out[:, 128 * n : 128 * n + 128].astype(BF16)
            dx[:, p] = more[:, 128 * n : 128 * n + 128]
        back_f = sel_f.astype(F32).T.astype(BF16)
        back_r = sel_r.astype(F32).T.astype(BF16)
        rho[...] += mat2(dj * yf, back_f) + mat2(dj * yr, back_r)
        kap[...] += mat2(wf * vf, back_f) + mat2(wr * vr, back_r)
        in_f = jnp.sum(state_f * adj_f, axis=0, keepdims=True)
        in_r = jnp.sum(state_r * adj_r, axis=0, keepdims=True)
        omega[...] += (exact_right(jnp.broadcast_to(in_f, (8, 256)), back_f)
                       + exact_right(jnp.broadcast_to(in_r, (8, 256)), back_r))
        for n, (left, cut) in enumerate(zip((ef * dj, er * dj, wf, wr), cuts)):
            hi, lo = split2(left)
            acc[n] += mat_nt(hi, jnp.concatenate(cut, axis=0))
            accl[n] += mat_nt(lo, cut[0])

    def arrive(i):
        @pl.when(i < 8)
        def _():
            receive(i)

        @pl.when(i > 0)
        def _():
            work(i - 1)

    loop(9, arrive)

    def total(n):
        a = acc[n]
        return a[:, :N] + a[:, N:] + accl[n]

    colsum = cs[...].T
    kappa = kap[...]
    through = rs[...] - colsum + rho[...]
    d_fall = jnp.where(
        lane < H,
        exact_left(ones_where(row <= col), through) + exact_left(ones_where(row > col), kappa),
        exact_left(ones_where(row >= col), through) + exact_left(ones_where(row < col), kappa),
    ) + omega[0:1, :] * jnp.exp(last)
    small = jnp.exp(-jnp.abs(z))
    soft = jnp.maximum(z, 0.0) + jnp.log1p(small)
    sigmoid = jnp.where(z >= 0.0, 1.0, small) / (1.0 + small)
    ratio = jnp.where(z < -30.0, 1.0, sigmoid / jnp.maximum(soft, 1e-30))
    ksi = xi[...]
    diag = step * ksi
    straight = colsum + kappa + sigma * diag
    dz = straight * ratio - rate * d_fall * sigmoid * keep
    dz = jnp.where(lane < 2 * H, dz, 0.0)

    ds_f = jnp.sum(jnp.where(lane < H, diag, 0.0), axis=1, keepdims=True)
    ds_r = jnp.sum(jnp.where((lane >= H) & (lane < 2 * H), diag, 0.0), axis=1, keepdims=True)
    mixing = dsc[...]
    turned = mixing.T
    eq = row == col
    m_f = jnp.where(eq, ds_f, jnp.where(row > col, mixing, 0.0))
    m_r = jnp.where(eq, ds_r, jnp.where(row < col, mixing, 0.0))
    mt_f = jnp.where(eq, ds_f, jnp.where(row < col, turned, 0.0))
    mt_r = jnp.where(eq, ds_r, jnp.where(row > col, turned, 0.0))
    d_bcf = jnp.concatenate([total(2) + mat3(mt_f, bcf[:, N:]), total(0) + mat3(m_f, bcf[:, :N])], axis=1)
    d_bcr = jnp.concatenate([total(3) + mat3(mt_r, bcr[:, N:]), total(1) + mat3(m_r, bcr[:, :N])], axis=1)
    dproj = jnp.concatenate([dz, d_bcf, d_bcr], axis=1)
    p_hi, p_lo = split2(dproj)
    p_cat = jnp.concatenate([p_hi, p_lo, p_hi], axis=1)

    r128 = iota((128, 128), 0)
    c128 = iota((128, 128), 1)
    fold = ones_where(((r128 < H) & (r128 == c128))
                      | ((r128 >= H) & (r128 < 2 * H) & (r128 + c128 == 2 * H - 1)))
    vectors = jnp.concatenate(
        [jnp.sum(dz, axis=0, keepdims=True),
         -jnp.sum(step * d_fall, axis=0, keepdims=True),
         jnp.sum(ksi, axis=0, keepdims=True),
         jnp.zeros((5, 128), F32)], axis=0)
    dz_t = dz.T
    f_t = jnp.concatenate([dz_t[0:H], d_bcf.T], axis=0)
    r_hi, r_lo = split2(jnp.concatenate([dz_t[H : 2 * H], d_bcr.T], axis=0))
    f_hi, f_lo = split2(f_t)

    def ordered(a):
        return jnp.concatenate([mat(rev, a[0:H]).astype(BF16), a[H:]], axis=0)

    left = jnp.concatenate(
        [jnp.concatenate([f_hi, ordered(r_hi)], axis=1),
         jnp.concatenate([f_lo, ordered(r_lo)], axis=1)], axis=0)

    def tile(n):
        return (n // tiles, n % tiles)

    def weights(j):
        i = lax.rem(j + (W // 2) * (1 - core), W)
        cols = pl.ds(pl.multiple_of(i * 256, 256), 256)
        far = pl.ds(pl.multiple_of((W - 1 - i) * 256, 256), 256)
        right = jnp.concatenate(
            [x_ref[:, cols], mat(x_ref[:, far], flip).astype(BF16)], axis=0)
        got = mat(left, right)
        got = got[0:160] + got[160:320]
        for n in range(2):
            for m in range(TILES):
                a, b = tile((2 * i + n) * TILES + m)
                grad[a, b] = got[8 * m : 8 * m + 8, 128 * n : 128 * n + 128]

    def blank(n):
        a, b = tile(n)
        grad[a, b] = jnp.zeros((8, 128), F32)

    loop(2 * plane * tiles, blank, TILES * G + 1)
    a, b = tile(TILES * G)
    grad[a, b] = exact_right(vectors, fold)

    def core_copy(k):
        return remote(grad.at[(1 - core) * plane + k], from_core.at[k],
                      s_core.at[k], r_core.at[k], partner)

    def plane_copy(k):
        return remote(held.at[k], from_plane.at[p_me], s_plane.at[k], r_plane.at[p_me],
                      plane_device(k))

    loop(W // 2 + 1, weights)
    loop(plane, lambda i: core_copy(plane_peer(i)).start())
    loop(W, weights, W // 2 + 1)

    def add_core(i):
        k = plane_peer(i)
        core_copy(k).wait_recv()
        held[k] = grad[core * plane + k] + from_core[k]

    def forward(i):
        add_core(i)
        plane_copy(plane_peer(i)).start()

    loop(plane - 1, forward)
    add_core(plane - 1)

    def sequence(i):
        cols = pl.ds(pl.multiple_of(i * 256, 256), 256)
        w_hi = whi[:, cols]
        w_cat = jnp.concatenate([w_hi, w_hi, wlo[:, cols]], axis=0)
        dseq_ref[:, cols] = (dx[:, cols] + mat(p_cat, w_cat)).astype(BF16)

    loop(W, sequence)
    part[...] = jnp.zeros(part.shape, F32)
    part[0:tiles] = held[p_me]

    def add_plane(i):
        k = lax.rem(p_me + plane - 1 - i, plane)
        remote(held.at[k], from_plane.at[k], s_plane.at[k], r_plane.at[k],
               plane_device(k)).wait_recv()
        part[0:tiles] += from_plane[k]

    loop(plane - 1, add_plane)

    def z_span(k):
        return pl.ds(k * zt, zt)

    def z_copy(k):
        return remote(part.at[z_span(k)], from_z.at[z_me], s_z.at[k], r_z.at[z_me], z_device(k))

    loop(depth - 1, lambda i: z_copy(z_peer(i)).start())
    full[z_span(z_me)] = part[z_span(z_me)]

    def add_z(i):
        k = z_peer(i)
        remote(part.at[z_span(k)], from_z.at[k], s_z.at[k], r_z.at[k], z_device(k)).wait_recv()
        full[z_span(z_me)] += from_z[k]

    loop(depth - 1, add_z)

    def z_share(k):
        return remote(full.at[z_span(z_me)], full.at[z_span(z_me)],
                      s_zg.at[k], r_zg.at[z_me], z_device(k))

    loop(depth - 1, lambda i: z_share(z_peer(i)).start())

    def z_got(i):
        k = z_peer(i)
        remote(full.at[z_span(k)], full.at[z_span(k)],
               s_zg.at[k], r_zg.at[k], z_device(k)).wait_recv()

    loop(depth - 1, z_got)
    mine = core * plane + p_me
    all_ref[mine] = full[0:tiles]

    def plane_share(k):
        return remote(all_ref.at[mine], all_ref.at[mine], s_pg.at[k], r_pg.at[p_me],
                      plane_device(k))

    def core_share(k):
        spot = all_ref.at[core * plane + k]
        return remote(spot, spot, s_cg.at[k], r_cg.at[k], partner)

    loop(plane - 1, lambda i: plane_share(plane_peer(i)).start())
    core_share(p_me).start()

    def plane_got(i):
        k = lax.rem(p_me + plane - 1 - i, plane)
        spot = all_ref.at[core * plane + k]
        remote(spot, spot, s_pg.at[k], r_pg.at[k], plane_device(k)).wait_recv()
        core_share(k).start()

    loop(plane - 1, plane_got)

    def core_got(k):
        spot = all_ref.at[(1 - core) * plane + k]
        remote(spot, spot, s_cg.at[k], r_cg.at[k], partner).wait_recv()

    loop(plane, core_got)

    def unpack(j):
        cols = pl.ds(pl.multiple_of(j * 128, 128), 128)
        for m in range(TILES):
            ref, base = (dt_ref, 0) if m < 4 else (b_ref, 4) if m < 12 else (c_ref, 12)
            a, b = tile(j * TILES + m)
            ref[8 * (m - base) : 8 * (m - base) + 8, cols] = all_ref[a, b]

    loop(G, unpack)
    a, b = tile(TILES * G)
    vec_ref[...] = all_ref[a, b]

    for r in range(2):
        loop(4, lambda q, r=r: swap(r, q).wait_send())
        loop(chips - 1, lambda i, r=r: to_chip(r, chip_peer(i)).wait_send())
        loop(PIECES - per, lambda i, r=r: to_owner(
            r, lax.rem((chip + 1) * per + i, PIECES)).wait_send())
    loop(8, lambda g: hand(g).wait_send())
    loop(plane, lambda k: core_copy(k).wait_send())
    loop(plane, lambda k: core_share(k).wait_send())
    loop(plane - 1, lambda i: plane_copy(plane_peer(i)).wait_send())
    loop(plane - 1, lambda i: plane_share(plane_peer(i)).wait_send())
    loop(depth - 1, lambda i: z_copy(z_peer(i)).wait_send())
    loop(depth - 1, lambda i: z_share(z_peer(i)).wait_send())


def sds(shape, dtype=F32):
    return jax.ShapeDtypeStruct(shape, dtype)


def on_device(sizes, sequence, n_blocks, w_dt, dt_bias, decay_rate, w_b, w_c, d_skip, cotangent):
    dps, ctxs = sizes
    chips = ctxs // 2
    halves = 2 if ctxs % 4 == 0 else 1
    depth = chips // halves
    plane = dps * halves
    tiles = -(-(TILES * G + 1) // (2 * plane))
    zt = -(-tiles // depth)
    per = PIECES // chips
    dma = pltpu.SemaphoreType.DMA

    def mem(*shape, dtype=F32):
        return pltpu.VMEM(shape, dtype)

    up, down = ROWS
    mixed, dseq, grad_dt, grad_b, grad_c, vectors = pl.pallas_call(
        functools.partial(kernel, chips, halves, depth),
        out_shape=[sds((T, D), BF16), sds((T, D), BF16),
                   sds((H, D)), sds((N, D)), sds((N, D)), sds((8, 128))],
        in_specs=[VMEM, VMEM, SMEM] + [VMEM] * 6,
        out_specs=[VMEM] * 6,
        scratch_shapes=[
            mem(384, D, dtype=BF16), mem(384, D, dtype=BF16), mem(128, T),
            mem(T, D), mem(T, D), mem(T, T), mem(T, 128), mem(128, T), mem(T, 128),
            mem(T, T), mem(T, 384, dtype=BF16),
            mem(T, 128), mem(T, 128), mem(8, 128), mem(4, T, 128), mem(4, T, N),
            mem(2, PIECES, up, 128), mem(2, PIECES, down, 128),
            mem(PIECES, up, 128), mem(PIECES, down, 128),
            mem(PIECES, up, 128), mem(PIECES, down, 128),
            mem(chips, per, up, 128), mem(chips, per, down, 128),
            mem(chips, per, 64, 128), mem(chips, per, 64, 128),
            mem(chips, per, 64, 128), mem(chips, per, 64, 128),
            mem(PIECES, 128, 128), mem(2, PIECES, 128, 128),
            mem(2 * plane, tiles, 8, 128), mem(2 * plane, tiles, 8, 128),
            mem(plane, tiles, 8, 128), mem(plane, tiles, 8, 128), mem(plane, tiles, 8, 128),
            mem(depth * zt, 8, 128), mem(depth, zt, 8, 128), mem(depth * zt, 8, 128),
            dma((2, 4)), dma((2, 4)), dma((2, PIECES)), dma((2, PIECES)),
            dma((2, chips)), dma((2, chips)), dma((8,)), dma((8,)),
        ] + [dma((plane,))] * 4 + [dma((depth,))] * 4 + [dma((plane,))] * 4,
        compiler_params=pltpu.CompilerParams(
            vmem_limit_bytes=ALL, collective_id=0, has_side_effects=True),
    )(sequence[0], cotangent[0], n_blocks, w_dt.T, w_b.T, w_c.T,
      dt_bias[None], decay_rate[None], d_skip[None])

    return (mixed[None], dseq[None], grad_dt.T, vectors[0, :H], vectors[1, :H],
            grad_b.T, grad_c.T, vectors[2, :H])


def solution(mesh):
    sizes = (mesh.shape["dp"], mesh.shape["ctx"])
    return jax.shard_map(
        functools.partial(on_device, sizes),
        mesh=mesh,
        in_specs=(
            P("dp", "ctx", None),
            P("dp", "ctx"),
            P(), P(), P(), P(), P(), P(),
            P("dp", "ctx", None),
        ),
        out_specs=(P("dp", "ctx", None), P("dp", "ctx", None), P(), P(), P(), P(), P(), P()),
        check_vma=False,
    )
```

time: 155 us -> 134 us (0.86)
  Pallas kernels: 147 us -> 125 us
    pallas_call x3 -> x1, Pallas kernels: 147 us -> 125 us  [on_device(): pl.pallas_call(functools.partial(kernel, chips, halves, depth), out_shape...]
    unnamed x9 -> x13, local copies, waits for them, and re-layouts: 6.92 us -> 6.64 us
where the time goes in v3:
time: 134 us
  Pallas kernels  125 us (93%)
  local copies, waits for them, and re-layouts  7.96 us (6%)
    pallas_call x1, Pallas kernels, on_device(): pl.pallas_call(functools.partial(kernel, chips, halves, depth), out_shape...  125 us
    unnamed x13, local copies, waits for them, and re-layouts  6.64 us

profile of v3, /device:TPU:1, one launch (start us, length us, event | category | flops | bytes accessed | tf_op | source)
XLA Modules:
  0.0 133.7 jit_solution(7811010969279777396)
XLA Ops:
  0.6 125.1 %shard_map.152 = (bf16[256,2048]{1,0:T(8,128)(2,1)}, bf16[256,2048]{1,0:T(8,128)(2,1)}, f32[32,2048]{1,0:T(8,128)}, f32[64,2048]{1,0:T(8,128)}, f32[64,2048]{1,0:T(8,128)}, /*index=5*/f32[8,128]{1,0:T(8,128)}) custom-call(bf16[256,2048]{1,0:T(8,128)(2,1)} %bitcast.19, bf16[256,2048]{1,0:T(8,128)(2,1)} %bitcast.20, s32[1,2]{1,0:T(1,128)} %nb_ref.1, ...), custom_call_target="tpu_custom_call" | custom-call | tf_op jit(solution)/shard_map/pallas_call | solution.py:788
  125.7 1.3 slice_bitcast_fusion
  127.0 0.0 copy-start
  127.0 2.4 %copy.22 = bf16[1,256,2048]{2,1,0:T(8,128)(2,1)} copy(bf16[1,256,2048]{2,1,0:T(8,128)(2,1)} %bitcast.22) | data formatting | bytes 2097152
  129.4 0.0 copy-done
  129.4 0.0 copy-start.3
  129.4 1.0 copy.23
  130.4 0.1 copy-done.3
  130.5 0.0 copy-start.2
  130.5 0.7 copy.24
  131.2 0.4 copy-done.2
  131.6 0.0 copy-start.1
  131.6 0.8 copy.25
  132.4 0.4 copy-done.1
  132.9 0.8 copy.26
Async XLA Ops:
  127.0 2.4 %copy-start = (bf16[256,2048]{1,0:T(8,128)(2,1)S(1)}, bf16[256,2048]{1,0:T(8,128)(2,1)}, u32[]{:S(2)}) copy-start(bf16[256,2048]{1,0:T(8,128)(2,1)} %get-tuple-element.15) | copy-start | bytes 3145732
  129.4 1.1 copy-start.3
  130.5 1.1 copy-start.2
  131.6 1.2 copy-start.1

commit v4 on v3

--- a/solution.py
+++ b/solution.py
@@ -24,7 +24,7 @@
 ROWS = (72, 64)
 TILES = 20
 FAR = -1e30
-EARLY = 12
+EARLY, LATER = 10, 13
 
 
 def iota(shape, axis):
@@ -199,16 +199,16 @@
     dx_ref[:, cols] = jnp.concatenate(dut, axis=0).T
 
 
-def kernel(chips, halves, depth, x_ref, dy_ref, nb_ref, wdt_ref, wb_ref, wc_ref,
+def kernel(halves, depth, x_ref, dy_ref, nb_ref, wdt_ref, wb_ref, wc_ref,
            bias_ref, rate_ref, skip_ref,
            mixed_ref, dseq_ref, dt_ref, b_ref, c_ref, vec_ref,
            whi, wlo, at_ref, y_in, dx, dsc, rs, cs, xi, sc, c3, rho, kap, omega, acc, accl,
            pack_up, pack_down, other_up, other_down, sums_up, sums_down, in_up, in_down,
-           out_up, out_down, came_up, came_down, give, carried,
+           out_up, out_down, came_up, came_down, give, carried, whole, begin,
            grad, all_ref, from_core, held, from_plane, part, from_z, full,
-           s_swap, r_swap, s_in, r_in, s_out, r_out, s_hand, r_hand,
+           s_swap, r_swap, s_in, r_in, s_out, r_out, s_half, r_half, s_hand, r_hand,
            s_core, r_core, s_plane, r_plane, s_z, r_z, s_zg, r_zg, s_pg, r_pg, s_cg, r_cg):
-    per = PIECES // chips
+    per = PIECES // depth
     pack, other = (pack_up, pack_down), (other_up, other_down)
     sums, inbox = (sums_up, sums_down), (in_up, in_down)
     outbox, came = (out_up, out_down), (came_up, came_down)
@@ -220,14 +220,9 @@
     core = ctx % 2
     chip = ctx // 2
     z_me = chip % depth
-    p_me = dp * halves + chip // depth
+    half_me = chip // depth
+    p_me = dp * halves + half_me
     partner = (dp, ctx + 1 - 2 * core)
-
-    def chip_device(k):
-        return (dp, 2 * k + core)
-
-    def chip_peer(i):
-        return lax.rem(chip + 1 + i, chips)
 
     def plane_device(k):
         return (k // halves, ((k % halves) * depth + z_me) * 2 + core)
@@ -236,7 +231,7 @@
         return lax.rem(p_me + 1 + i, plane)
 
     def z_device(k):
-        return (dp, ((chip // depth) * depth + k) * 2 + core)
+        return (dp, (half_me * depth + k) * 2 + core)
 
     def z_peer(i):
         return lax.rem(z_me + 1 + i, depth)
@@ -256,8 +251,8 @@
 
     barrier = pltpu.get_barrier_semaphore()
     pl.semaphore_signal(barrier, inc=1, device_id=partner, device_id_type=MESH)
-    loop(chips - 1, lambda i: pl.semaphore_signal(
-        barrier, inc=1, device_id=chip_device(chip_peer(i)), device_id_type=MESH))
+    loop(depth - 1, lambda i: pl.semaphore_signal(
+        barrier, inc=1, device_id=z_device(z_peer(i)), device_id_type=MESH))
     loop(plane - 1, lambda i: pl.semaphore_signal(
         barrier, inc=1, device_id=plane_device(plane_peer(i)), device_id_type=MESH))
 
@@ -323,19 +318,20 @@
     first = (core == 0, core == 1)
 
     def block(i):
-        return lax.rem(i + chip * per // 4, 4)
+        return lax.rem(i + z_me * per // 4, 4)
 
     def swap(r, q):
         spot = pl.ds(4 * q, 4)
         return remote(pack[r].at[1 - core, spot], other[r].at[spot],
                       s_swap.at[r, q], r_swap.at[r, q], partner)
 
-    def to_owner(r, p):
-        return remote(sums[r].at[p, pl.ds(0, ROWS[r])], in_piece(r, chip, p % per),
-                      s_in.at[r, p], r_in.at[r, chip * per + p % per], chip_device(p // per))
-
-    def in_piece(r, k, u):
-        return inbox[r].at[k, u]
+    def slot(k, g):
+        return k * (per // 2) + g % (per // 2)
+
+    def to_owner(r, g):
+        return remote(sums[r].at[pl.ds(2 * g, 2), pl.ds(0, ROWS[r])],
+                      inbox[r].at[z_me, pl.ds(2 * g % per, 2)],
+                      s_in.at[r, g], r_in.at[r, slot(z_me, g)], z_device(2 * g // per))
 
     def local_states(r, half, q):
         i = 4 * half + q
@@ -371,31 +367,35 @@
 
     def add_up(r, q):
         swap(r, q).wait_recv()
-        for n in range(4):
-            p = 4 * q + n
-            own = p // per == chip
-            drops = drop_rows(r, p)
-            out = []
-            for s in range(2):
-                rows = slice(32 * s, 32 * s + 32)
-                dm, dt = drops[s]
-                mine = pack[r][core, p, rows, :]
-                theirs = other[r][p, rows, :]
-                out.append(jnp.where(first[r], dt * mine + theirs, dm * theirs + mine))
-            if r == 0:
-                out.append(pack_up[core, p, 64:72, :] * other_up[p, 64:72, :])
-            whole = jnp.concatenate(out, axis=0)
+        for n in range(2):
+            g = 2 * q + n
+            own = 2 * g // per == z_me
+            both_pieces = []
+            for p in (2 * g, 2 * g + 1):
+                drops = drop_rows(r, p)
+                out = []
+                for s in range(2):
+                    rows = slice(32 * s, 32 * s + 32)
+                    dm, dt = drops[s]
+                    mine = pack[r][core, p, rows, :]
+                    theirs = other[r][p, rows, :]
+                    out.append(jnp.where(first[r], dt * mine + theirs, dm * theirs + mine))
+                if r == 0:
+                    out.append(pack_up[core, p, 64:72, :] * other_up[p, 64:72, :])
+                both_pieces.append(jnp.concatenate(out, axis=0))
 
             @pl.when(own)
             def _():
-                inbox[r][chip, p % per] = whole
+                for h in range(2):
+                    inbox[r][z_me, 2 * g % per + h] = both_pieces[h]
 
             @pl.when(jnp.logical_not(own))
             def _():
-                sums[r][p] = whole
-                to_owner(r, p).start()
-
-    pl.semaphore_wait(barrier, plane + chips - 1)
+                for h in range(2):
+                    sums[r][2 * g + h] = both_pieces[h]
+                to_owner(r, g).start()
+
+    pl.semaphore_wait(barrier, plane + depth - 1)
     for r in range(2):
         def states(i, r=r):
             @pl.when(i < 4)
@@ -422,38 +422,67 @@
         inner_pair(i, x_ref, dy_ref, at_ref, sc, c3, y_in, dx, dsc, rs, cs, xi)
 
     def to_chip(r, k):
-        return remote(outbox[r].at[k], came[r].at[chip],
-                      s_out.at[r, k], r_out.at[r, chip], chip_device(k))
+        return remote(outbox[r].at[k], came[r].at[z_me],
+                      s_out.at[r, k], r_out.at[r, z_me], z_device(k))
+
+    def across(r):
+        return remote(whole.at[r], begin.at[r], s_half.at[r], r_half.at[r],
+                      (dp, ((1 - half_me) * depth + z_me) * 2 + core))
 
     def scan(r):
-        def arrived(i):
-            k = chip_peer(i)
-            for u in range(per):
-                remote(sums[r].at[k * per + u, pl.ds(0, ROWS[r])], in_piece(r, k, u),
-                       s_in.at[r, k * per + u], r_in.at[r, k * per + u],
-                       chip_device(k)).wait_recv()
-
-        loop(chips - 1, arrived)
-
         def piece(u):
             def turn(i, run):
-                k = i if r == 0 else chips - 1 - i
+                k = i if r == 0 else depth - 1 - i
                 outbox[r][k, u] = run
                 drop = in_up[k, u, 64:72, :]
                 one, two = (drop[0:1], drop[1:2]) if r == 0 else (drop[1:2], drop[0:1])
                 return (jnp.concatenate([one * run[0:32], two * run[32:64]], axis=0)
                         + inbox[r][k, u, 0:64, :])
 
-            lax.fori_loop(0, chips, turn, jnp.zeros((64, 128), F32))
+            whole[r, u] = lax.fori_loop(0, depth, turn, begin[r, u])
 
         loop(per, piece)
-        loop(chips - 1, lambda i: to_chip(r, chip_peer(i)).start())
-        came[r][chip] = outbox[r][chip]
+
+    def scatter(r):
+        loop(depth - 1, lambda i: to_chip(r, z_peer(i)).start())
+        came[r][z_me] = outbox[r][z_me]
+
+    def gives(r):
+        return half_me == (0 if r == 0 else halves - 1)
+
+    def collect(r):
+        def arrived(i):
+            k = z_peer(i)
+            for n in range(per // 2):
+                g = k * (per // 2) + n
+                remote(sums[r].at[pl.ds(2 * g, 2), pl.ds(0, ROWS[r])],
+                       inbox[r].at[k, pl.ds(2 * n, 2)],
+                       s_in.at[r, g], r_in.at[r, g], z_device(k)).wait_recv()
+
+        loop(depth - 1, arrived)
+
+        @pl.when(gives(r))
+        def _():
+            begin[r] = jnp.zeros((per, 64, 128), F32)
+            scan(r)
+            if halves == 2:
+                across(r).start()
+            scatter(r)
+
+    def finish(r):
+        @pl.when(jnp.logical_not(gives(r)))
+        def _():
+            across(r).wait_recv()
+            scan(r)
+            scatter(r)
 
     loop(EARLY, inner)
-    scan(0)
-    loop(G, inner, EARLY)
-    scan(1)
+    collect(0)
+    loop(LATER, inner, EARLY)
+    finish(0)
+    loop(G, inner, LATER)
+    collect(1)
+    finish(1)
 
     sig_f = jnp.sum(bcf[:, :N] * bcf[:, N:], axis=1, keepdims=True)
     sig_r = jnp.sum(bcr[:, :N] * bcr[:, N:], axis=1, keepdims=True)
@@ -468,39 +497,42 @@
     l_br, l_cr = left3(bcr[:, :N]), left3(bcr[:, N:])
 
     def group_of(i):
-        return lax.rem(chip * per // 2 + i, 8)
-
-    def hand(g):
+        return lax.rem(z_me * per // 2 + i, 8)
+
+    def hand(r, g):
         spot = pl.ds(2 * g, 2)
-        return remote(give.at[spot], carried.at[core, spot], s_hand.at[g], r_hand.at[g], partner)
-
-    def receive(i):
+        rows = pl.ds(64 * r, 64)
+        return remote(give.at[spot, rows], carried.at[core, spot, rows],
+                      s_hand.at[r, g], r_hand.at[r, g], partner)
+
+    def receive(r, i):
         g = group_of(i)
-        for n in range(2):
-            p = 2 * g + n
-            k = p // per
-            for r in range(2):
-                @pl.when((k != chip) & (p % per == 0))
-                def _():
-                    remote(outbox[r].at[k], came[r].at[k], s_out.at[r, k], r_out.at[r, k],
-                           chip_device(k)).wait_recv()
-
-                drops = drop_rows(r, p)
-                for s in range(2):
-                    rows = slice(32 * s, 32 * s + 32)
-                    to = slice(64 * r + 32 * s, 64 * r + 32 * s + 32)
-                    dm, dt = drops[s]
-                    got = came[r][k, p % per, rows, :]
-                    mine = pack[r][core, p, rows, :]
-                    theirs = other[r][p, rows, :]
-                    carried[core, p, to, :] = jnp.where(first[r], got, dt * got + theirs)
-                    give[p, to, :] = jnp.where(first[r], dm * got + mine, got)
-        hand(g).start()
-
-    def work(i):
+        k = 2 * g // per
+
+        @pl.when((k != z_me) & (2 * g % per == 0))
+        def _():
+            remote(outbox[r].at[k], came[r].at[k], s_out.at[r, k], r_out.at[r, k],
+                   z_device(k)).wait_recv()
+
+        for p in (2 * g, 2 * g + 1):
+            drops = drop_rows(r, p)
+            for s in range(2):
+                rows = slice(32 * s, 32 * s + 32)
+                to = slice(64 * r + 32 * s, 64 * r + 32 * s + 32)
+                dm, dt = drops[s]
+                got = came[r][k, p % per, rows, :]
+                mine = pack[r][core, p, rows, :]
+                theirs = other[r][p, rows, :]
+                carried[core, p, to, :] = jnp.where(first[r], got, dt * got + theirs)
+                give[p, to, :] = jnp.where(first[r], dm * got + mine, got)
+        hand(r, g).start()
+
+    def work(r, i):
         g = group_of(i)
-        remote(give.at[pl.ds(2 * g, 2)], carried.at[1 - core, pl.ds(2 * g, 2)],
-               s_hand.at[g], r_hand.at[g], partner).wait_recv()
+        spot = pl.ds(2 * g, 2)
+        span = pl.ds(64 * r, 64)
+        remote(give.at[spot, span], carried.at[1 - core, spot, span],
+               s_hand.at[r, g], r_hand.at[r, g], partner).wait_recv()
         groups = (8 * core + g, 8 * (1 - core) + g)
         places = [pl.ds(pl.multiple_of(j * 128, 128), 128) for j in groups]
 
@@ -513,53 +545,59 @@
                 [jnp.concatenate([carried[h, 2 * g, rows, :], carried[h, 2 * g + 1, rows, :]], axis=0)
                  for h in (core, 1 - core)], axis=1)
 
-        state_f, adj_r, state_r, adj_f = state(0), state(1), state(2), state(3)
-        sel_f, sel_r = spread(*groups)
-        two_f, two_r = twice(sel_f), twice(sel_r)
-        ef, er = mat(e2, two_f), mat(e2, two_r)
-        tf, tr = mat(tail2, two_f), mat(tail2, two_r)
-        one = sel_f + sel_r
-        coef = mat(coef3, jnp.concatenate([one, one, one], axis=0))
+        now, adj = state(2 * r), state(2 * r + 1)
+        sel = spread(*groups)
+        sel_s, sel_a = sel[r], sel[1 - r]
+        e = mat(e2, twice(sel_s))
+        t = mat(tail2, twice(sel_a))
         xj = wide(x_ref).astype(F32)
         dj = wide(dy_ref).astype(F32)
-        wf, wr = tf * xj, tr * xj
-        cuts = [split2(a) for a in (state_f, state_r, adj_f, adj_r)]
+        w = t * xj
+        cut_s, cut_a = split2(now), split2(adj)
 
         def times(left, cut):
             return mat(left, jnp.concatenate([cut[0], cut[0], cut[1]], axis=0))
 
-        yf = ef * times(l_cf, cuts[0])
-        yr = er * times(l_cr, cuts[1])
-        vf = times(l_bf, cuts[2])
-        vr = times(l_br, cuts[3])
-        out = wide(y_in) + (yf + yr) + coef * xj
-        more = wide(dx) + (tf * vf + tr * vr) + coef * dj
+        y = e * times((l_cf, l_cr)[r], cut_s)
+        v = times((l_br, l_bf)[r], cut_a)
+        out = wide(y_in) + y
+        more = wide(dx) + t * v
+        if r == 0:
+            one = sel[0] + sel[1]
+            coef = mat(coef3, jnp.concatenate([one, one, one], axis=0))
+            out = out + coef * xj
+            more = more + coef * dj
         for n, p in enumerate(places):
-            mixed_ref[:, p] = out[:, 128 * n : 128 * n + 128].astype(BF16)
+            part_out = out[:, 128 * n : 128 * n + 128]
+            if r == 0:
+                y_in[:, p] = part_out
+            else:
+                mixed_ref[:, p] = part_out.astype(BF16)
             dx[:, p] = more[:, 128 * n : 128 * n + 128]
-        back_f = sel_f.astype(F32).T.astype(BF16)
-        back_r = sel_r.astype(F32).T.astype(BF16)
-        rho[...] += mat2(dj * yf, back_f) + mat2(dj * yr, back_r)
-        kap[...] += mat2(wf * vf, back_f) + mat2(wr * vr, back_r)
-        in_f = jnp.sum(state_f * adj_f, axis=0, keepdims=True)
-        in_r = jnp.sum(state_r * adj_r, axis=0, keepdims=True)
-        omega[...] += (exact_right(jnp.broadcast_to(in_f, (8, 256)), back_f)
-                       + exact_right(jnp.broadcast_to(in_r, (8, 256)), back_r))
-        for n, (left, cut) in enumerate(zip((ef * dj, er * dj, wf, wr), cuts)):
+        back = [a.astype(F32).T.astype(BF16) for a in sel]
+        rho[...] += mat2(dj * y, back[r])
+        kap[...] += mat2(w * v, back[1 - r])
+        if r == 1:
+            in_f = jnp.sum(state(0) * adj, axis=0, keepdims=True)
+            in_r = jnp.sum(now * state(1), axis=0, keepdims=True)
+            omega[...] += (exact_right(jnp.broadcast_to(in_f, (8, 256)), back[0])
+                           + exact_right(jnp.broadcast_to(in_r, (8, 256)), back[1]))
+        for n, left, cut in ((r, e * dj, cut_s), (3 - r, w, cut_a)):
             hi, lo = split2(left)
             acc[n] += mat_nt(hi, jnp.concatenate(cut, axis=0))
             accl[n] += mat_nt(lo, cut[0])
 
-    def arrive(i):
-        @pl.when(i < 8)
-        def _():
-            receive(i)
-
-        @pl.when(i > 0)
-        def _():
-            work(i - 1)
-
-    loop(9, arrive)
+    for r in range(2):
+        def arrive(i, r=r):
+            @pl.when(i < 8)
+            def _():
+                receive(r, i)
+
+            @pl.when(i > 0)
+            def _():
+                work(r, i - 1)
+
+        loop(9, arrive)
 
     def total(n):
         a = acc[n]
@@ -754,16 +792,36 @@
 
     for r in range(2):
         loop(4, lambda q, r=r: swap(r, q).wait_send())
-        loop(chips - 1, lambda i, r=r: to_chip(r, chip_peer(i)).wait_send())
-        loop(PIECES - per, lambda i, r=r: to_owner(
-            r, lax.rem((chip + 1) * per + i, PIECES)).wait_send())
-    loop(8, lambda g: hand(g).wait_send())
+        loop(8, lambda g, r=r: hand(r, g).wait_send())
+        loop(depth - 1, lambda i, r=r: to_chip(r, z_peer(i)).wait_send())
+        loop(8 - per // 2, lambda i, r=r: to_owner(
+            r, lax.rem((z_me + 1) * (per // 2) + i, 8)).wait_send())
+        if halves == 2:
+            pl.when(gives(r))(lambda r=r: across(r).wait_send())
     loop(plane, lambda k: core_copy(k).wait_send())
     loop(plane, lambda k: core_share(k).wait_send())
     loop(plane - 1, lambda i: plane_copy(plane_peer(i)).wait_send())
     loop(plane - 1, lambda i: plane_share(plane_peer(i)).wait_send())
     loop(depth - 1, lambda i: z_copy(z_peer(i)).wait_send())
     loop(depth - 1, lambda i: z_share(z_peer(i)).wait_send())
+
+
+def deliver_kernel(*refs):
+    sources, vec_ref = refs[0:5], refs[5]
+    targets, rows, holds, sems_in, sems = refs[6:11], refs[11:14], refs[14:19], refs[19], refs[20]
+    copies_in = [pltpu.make_async_copy(a, b, sems_in.at[n])
+                 for n, (a, b) in enumerate(zip(sources, holds))]
+    copies = [pltpu.make_async_copy(a, b, sems.at[n])
+              for n, (a, b) in enumerate(zip(holds, targets))]
+    for copy in copies_in:
+        copy.start()
+    for copy_in, copy in zip(copies_in, copies):
+        copy_in.wait()
+        copy.start()
+    for n, row in enumerate(rows):
+        row[...] = vec_ref[n : n + 1, 0:H]
+    for copy in copies:
+        copy.wait()
 
 
 def sds(shape, dtype=F32):
@@ -778,15 +836,15 @@
     plane = dps * halves
     tiles = -(-(TILES * G + 1) // (2 * plane))
     zt = -(-tiles // depth)
-    per = PIECES // chips
+    per = PIECES // depth
     dma = pltpu.SemaphoreType.DMA
 
     def mem(*shape, dtype=F32):
         return pltpu.VMEM(shape, dtype)
 
     up, down = ROWS
-    mixed, dseq, grad_dt, grad_b, grad_c, vectors = pl.pallas_call(
-        functools.partial(kernel, chips, halves, depth),
+    results = pl.pallas_call(
+        functools.partial(kernel, halves, depth),
         out_shape=[sds((T, D), BF16), sds((T, D), BF16),
                    sds((H, D)), sds((N, D)), sds((N, D)), sds((8, 128))],
         in_specs=[VMEM, VMEM, SMEM] + [VMEM] * 6,
@@ -799,23 +857,34 @@
             mem(2, PIECES, up, 128), mem(2, PIECES, down, 128),
             mem(PIECES, up, 128), mem(PIECES, down, 128),
             mem(PIECES, up, 128), mem(PIECES, down, 128),
-            mem(chips, per, up, 128), mem(chips, per, down, 128),
-            mem(chips, per, 64, 128), mem(chips, per, 64, 128),
-            mem(chips, per, 64, 128), mem(chips, per, 64, 128),
+            mem(depth, per, up, 128), mem(depth, per, down, 128),
+            mem(depth, per, 64, 128), mem(depth, per, 64, 128),
+            mem(depth, per, 64, 128), mem(depth, per, 64, 128),
             mem(PIECES, 128, 128), mem(2, PIECES, 128, 128),
+            mem(2, per, 64, 128), mem(2, per, 64, 128),
             mem(2 * plane, tiles, 8, 128), mem(2 * plane, tiles, 8, 128),
             mem(plane, tiles, 8, 128), mem(plane, tiles, 8, 128), mem(plane, tiles, 8, 128),
             mem(depth * zt, 8, 128), mem(depth, zt, 8, 128), mem(depth * zt, 8, 128),
-            dma((2, 4)), dma((2, 4)), dma((2, PIECES)), dma((2, PIECES)),
-            dma((2, chips)), dma((2, chips)), dma((8,)), dma((8,)),
+            dma((2, 4)), dma((2, 4)), dma((2, 8)), dma((2, 8)),
+            dma((2, depth)), dma((2, depth)), dma((2,)), dma((2,)), dma((2, 8)), dma((2, 8)),
         ] + [dma((plane,))] * 4 + [dma((depth,))] * 4 + [dma((plane,))] * 4,
         compiler_params=pltpu.CompilerParams(
             vmem_limit_bytes=ALL, collective_id=0, has_side_effects=True),
     )(sequence[0], cotangent[0], n_blocks, w_dt.T, w_b.T, w_c.T,
       dt_bias[None], decay_rate[None], d_skip[None])
 
-    return (mixed[None], dseq[None], grad_dt.T, vectors[0, :H], vectors[1, :H],
-            grad_b.T, grad_c.T, vectors[2, :H])
+    anywhere = pl.BlockSpec(memory_space=pl.ANY)
+    mixed, dseq, grad_dt, grad_b, grad_c, bias, rate, skip = pl.pallas_call(
+        deliver_kernel,
+        out_shape=[sds(a.shape, a.dtype) for a in results[0:5]] + [sds((1, H))] * 3,
+        in_specs=[anywhere] * 5 + [VMEM],
+        out_specs=[anywhere] * 5 + [VMEM] * 3,
+        scratch_shapes=[mem(*a.shape, dtype=a.dtype) for a in results[0:5]] + [dma((5,)), dma((5,))],
+        compiler_params=pltpu.CompilerParams(vmem_limit_bytes=ALL),
+    )(*results)
+
+    return (mixed[None], dseq[None], grad_dt.T, bias[0], rate[0],
+            grad_b.T, grad_c.T, skip[0])
 
 
 def solution(mesh):

time: 134 us -> 126 us (0.940)
  local copies, waits for them, and re-layouts: 7.96 us -> 0 us
    unnamed x13 -> x0, local copies, waits for them, and re-layouts: 6.64 us -> none
    pallas_call x1 -> x2, Pallas kernels: 125 us -> 125 us  [the longest x1 121 us: on_device(): pl.pallas_call(functools.partial(kernel, halves, depth), out_shape=[sds((...]
where the time goes in v4:
time: 126 us
  Pallas kernels  125 us (99%)
    pallas_call x1, Pallas kernels, on_device(): pl.pallas_call(functools.partial(kernel, halves, depth), out_shape=[sds((...  121 us
    pallas_call x1, Pallas kernels, on_device(): pl.pallas_call(deliver_kernel, out_shape=[sds(a.shape, a.dtype) for a in...  4.26 us

profile of v4, /device:TPU:1, one launch (start us, length us, event | category | flops | bytes accessed | tf_op | source)
XLA Modules:
  0.0 126.0 jit_solution(10653729576195191477)
XLA Ops:
  0.6 121.1 %shard_map.152 = (bf16[256,2048]{1,0:T(8,128)(2,1)}, bf16[256,2048]{1,0:T(8,128)(2,1)}, f32[32,2048]{1,0:T(8,128)}, f32[64,2048]{1,0:T(8,128)}, f32[64,2048]{1,0:T(8,128)}, /*index=5*/f32[8,128]{1,0:T(8,128)}) custom-call(bf16[256,2048]{1,0:T(8,128)(2,1)} %bitcast.16, bf16[256,2048]{1,0:T(8,128)(2,1)} %bitcast.17, s32[1,2]{1,0:T(1,128)} %nb_ref.1, ...), custom_call_target="tpu_custom_call" | custom-call | tf_op jit(solution)/shard_map/pallas_call | solution.py:846
  121.7 4.3 %shard_map.153 = (bf16[256,2048]{1,0:T(8,128)(2,1)}, bf16[256,2048]{1,0:T(8,128)(2,1)}, f32[32,2048]{1,0:T(8,128)}, f32[64,2048]{1,0:T(8,128)}, f32[64,2048]{1,0...) custom-call(bf16[256,2048]{1,0:T(8,128)(2,1)} %get-tuple-element.22.refs_0_, ...), custom_call_target="tpu_custom_call" | custom-call | tf_op jit(solution)/shard_map/pallas_call | solution.py:877

commit v5 on v4

--- a/solution.py
+++ b/solution.py
@@ -587,6 +587,20 @@
             acc[n] += mat_nt(hi, jnp.concatenate(cut, axis=0))
             accl[n] += mat_nt(lo, cut[0])
 
+    ksi = xi[...]
+    diag = step * ksi
+    ds_f = jnp.sum(jnp.where(lane < H, diag, 0.0), axis=1, keepdims=True)
+    ds_r = jnp.sum(jnp.where((lane >= H) & (lane < 2 * H), diag, 0.0), axis=1, keepdims=True)
+    mixing = dsc[...]
+    turned = mixing.T
+    eq = row == col
+    m_f = jnp.where(eq, ds_f, jnp.where(row > col, mixing, 0.0))
+    m_r = jnp.where(eq, ds_r, jnp.where(row < col, mixing, 0.0))
+    mt_f = jnp.where(eq, ds_f, jnp.where(row < col, turned, 0.0))
+    mt_r = jnp.where(eq, ds_r, jnp.where(row > col, turned, 0.0))
+    own_bf, own_cf = mat3(mt_f, bcf[:, N:]), mat3(m_f, bcf[:, :N])
+    own_br, own_cr = mat3(mt_r, bcr[:, N:]), mat3(m_r, bcr[:, :N])
+
     for r in range(2):
         def arrive(i, r=r):
             @pl.when(i < 8)
@@ -615,23 +629,12 @@
     soft = jnp.maximum(z, 0.0) + jnp.log1p(small)
     sigmoid = jnp.where(z >= 0.0, 1.0, small) / (1.0 + small)
     ratio = jnp.where(z < -30.0, 1.0, sigmoid / jnp.maximum(soft, 1e-30))
-    ksi = xi[...]
-    diag = step * ksi
     straight = colsum + kappa + sigma * diag
     dz = straight * ratio - rate * d_fall * sigmoid * keep
     dz = jnp.where(lane < 2 * H, dz, 0.0)
 
-    ds_f = jnp.sum(jnp.where(lane < H, diag, 0.0), axis=1, keepdims=True)
-    ds_r = jnp.sum(jnp.where((lane >= H) & (lane < 2 * H), diag, 0.0), axis=1, keepdims=True)
-    mixing = dsc[...]
-    turned = mixing.T
-    eq = row == col
-    m_f = jnp.where(eq, ds_f, jnp.where(row > col, mixing, 0.0))
-    m_r = jnp.where(eq, ds_r, jnp.where(row < col, mixing, 0.0))
-    mt_f = jnp.where(eq, ds_f, jnp.where(row < col, turned, 0.0))
-    mt_r = jnp.where(eq, ds_r, jnp.where(row > col, turned, 0.0))
-    d_bcf = jnp.concatenate([total(2) + mat3(mt_f, bcf[:, N:]), total(0) + mat3(m_f, bcf[:, :N])], axis=1)
-    d_bcr = jnp.concatenate([total(3) + mat3(mt_r, bcr[:, N:]), total(1) + mat3(m_r, bcr[:, :N])], axis=1)
+    d_bcf = jnp.concatenate([total(2) + own_bf, total(0) + own_cf], axis=1)
+    d_bcr = jnp.concatenate([total(3) + own_br, total(1) + own_cr], axis=1)
     dproj = jnp.concatenate([dz, d_bcf, d_bcr], axis=1)
     p_hi, p_lo = split2(dproj)
     p_cat = jnp.concatenate([p_hi, p_lo, p_hi], axis=1)

time: 126 us -> 126 us (level)
  no operation moved by 1% of the time
where the time goes in v5:
time: 126 us
  Pallas kernels  125 us (99%)
    pallas_call x1, Pallas kernels, on_device(): pl.pallas_call(functools.partial(kernel, halves, depth), out_shape=[sds((...  121 us
    pallas_call x1, Pallas kernels, on_device(): pl.pallas_call(deliver_kernel, out_shape=[sds(a.shape, a.dtype) for a in...  4.26 us

profile of v5, /device:TPU:1, one launch (start us, length us, event | category | flops | bytes accessed | tf_op | source)
XLA Modules:
  0.0 125.5 jit_solution(14240414518176568237)
XLA Ops:
  0.6 120.6 %shard_map.152 = (bf16[256,2048]{1,0:T(8,128)(2,1)}, bf16[256,2048]{1,0:T(8,128)(2,1)}, f32[32,2048]{1,0:T(8,128)}, f32[64,2048]{1,0:T(8,128)}, f32[64,2048]{1,0:T(8,128)}, /*index=5*/f32[8,128]{1,0:T(8,128)}) custom-call(bf16[256,2048]{1,0:T(8,128)(2,1)} %bitcast.16, bf16[256,2048]{1,0:T(8,128)(2,1)} %bitcast.17, s32[1,2]{1,0:T(1,128)} %nb_ref.1, ...), custom_call_target="tpu_custom_call" | custom-call | tf_op jit(solution)/shard_map/pallas_call | solution.py:849
  121.3 4.3 %shard_map.153 = (bf16[256,2048]{1,0:T(8,128)(2,1)}, bf16[256,2048]{1,0:T(8,128)(2,1)}, f32[32,2048]{1,0:T(8,128)}, f32[64,2048]{1,0:T(8,128)}, f32[64,2048]{1,0...) custom-call(bf16[256,2048]{1,0:T(8,128)(2,1)} %get-tuple-element.22.refs_0_, ...), custom_call_target="tpu_custom_call" | custom-call | tf_op jit(solution)/shard_map/pallas_call | solution.py:880
